TPU v7x, 256 devices: a whole 4x4x8 slice. The times are simulated.
256 devices in a mesh: dp: 2 (over core), seq: 16 (over y, x), exp: 8 (over z).
Axes of the slice: x: 4, y: 4, z: 8, core: 2. Of those that a mesh axis runs over, the one named last changes fastest.
Arguments:
- query: bfloat16 [16, 2048, 2048], P(('dp', 'exp'), 'seq'), may hold values from -96 to 96
- keys: bfloat16 [16, 2048, 256], P(('dp', 'exp'), 'seq'), may hold values from -6 to 6
- values: bfloat16 [16, 2048, 256], P(('dp', 'exp'), 'seq'), may hold values from -6 to 6
- sinks: float32 [32], replicated, may hold values from -1 to 3
- attn_grad: bfloat16 [16, 2048, 2048], P(('dp', 'exp'), 'seq'), may hold values from -6 to 6
- moe_in: bfloat16 [16, 2048, 2880], P(('dp', 'exp'), 'seq'), may hold values from -6 to 6
- moe_grad: bfloat16 [16, 2048, 2880], P(('dp', 'exp'), 'seq'), may hold values from -6 to 6
- expert_ids: int32 [16, 2048, 4], P(('dp', 'exp'), 'seq'), may hold values from 0 to 127, all different within a row
- route_weights: float32 [16, 2048, 4], P(('dp', 'exp'), 'seq'), may hold values from 0.1 to 0.6
- w_gate_up: bfloat16 [8, 2880, 2, 2880], P('exp', None, None, 'seq'), may hold values from -0.109375 to 0.109375
- w_down: bfloat16 [8, 2880, 2880], P('exp', 'seq'), may hold values from -0.109375 to 0.109375
Outputs:
- attn_out: bfloat16 [16, 2048, 2048], P(('dp', 'exp'), 'seq')
- d_query: bfloat16 [16, 2048, 2048], P(('dp', 'exp'), 'seq')
- d_keys: bfloat16 [16, 2048, 256], P(('dp', 'exp'), 'seq')
- d_values: bfloat16 [16, 2048, 256], P(('dp', 'exp'), 'seq')
- d_sinks: float32 [32], replicated
- moe_out: bfloat16 [16, 2048, 2880], P(('dp', 'exp'), 'seq')
- d_moe_in: bfloat16 [16, 2048, 2880], P(('dp', 'exp'), 'seq')
- d_gate_up: bfloat16 [8, 2880, 2, 2880], P('exp', None, None, 'seq')
- d_down: bfloat16 [8, 2880, 2880], P('exp', 'seq')
Inputs may be any that keep to these rules, and one draw needn't show every extreme that they name: `expert_ids`: the 4 ids of a token differ.
All inputs are finite; a program needn't handle non-finite values.
Results may differ from a plain program's by a relative error of at most 0.024.
Values may be sent and summed in bfloat16 or wider, within the bound.
A program may use at most 128 MiB of HBM per device.

v0:
```python
import math

import jax
import jax.numpy as jnp
from jax import lax
from jax.sharding import PartitionSpec as P

D = 2880
HQ = 32
HK = 4
HD = 64
TOP = 4
CAP = 4


ROPE_BASE = 150000.0
YARN_FACTOR = 32.0
YARN_INITIAL = 4096.0
BETA_FAST = 32.0
BETA_SLOW = 1.0
SWIGLU_ALPHA = 1.702
SCORE_SCALE = 0.125


def rotary_tables(seq_rows):
    half_size = HD // 2
    steps_f = jnp.arange(half_size, dtype=jnp.float32)
    powers = jnp.exp(steps_f * (2.0 * math.log(ROPE_BASE) / HD))
    extrap_freq = 1.0 / powers
    interp_freq = extrap_freq / YARN_FACTOR
    low_end = (
        HD * math.log(YARN_INITIAL / (BETA_FAST * 2.0 * math.pi)) / (2.0 * math.log(ROPE_BASE))
    )
    high_end = (
        HD * math.log(YARN_INITIAL / (BETA_SLOW * 2.0 * math.pi)) / (2.0 * math.log(ROPE_BASE))
    )
    ramp_val = jnp.clip((steps_f - low_end) / (high_end - low_end), 0.0, 1.0)
    inv_freq = interp_freq * ramp_val + extrap_freq * (1.0 - ramp_val)
    concentration = 0.1 * math.log(YARN_FACTOR) + 1.0
    angles = jnp.arange(seq_rows, dtype=jnp.float32)[:, None] * inv_freq[None, :]
    return (jnp.cos(angles) * concentration, jnp.sin(angles) * concentration)


def rotate(values_in, cos_table, sin_table):
    half_size = values_in.shape[-1] // 2
    first_half = values_in[..., :half_size]
    second_half = values_in[..., half_size:]
    cos_b = cos_table[:, None, :]
    sin_b = sin_table[:, None, :]
    return jnp.concatenate(
        [first_half * cos_b - second_half * sin_b, second_half * cos_b + first_half * sin_b],
        axis=-1,
    )


def unrotate(values_in, cos_table, sin_table):
    half_size = values_in.shape[-1] // 2
    first_half = values_in[..., :half_size]
    second_half = values_in[..., half_size:]
    cos_b = cos_table[:, None, :]
    sin_b = sin_table[:, None, :]
    return jnp.concatenate(
        [first_half * cos_b + second_half * sin_b, second_half * cos_b - first_half * sin_b],
        axis=-1,
    )


def attention_here(q_heads, k_head, v_head, g_heads, sink_here, cos_table, sin_table):
    seq_rows = q_heads.shape[0]
    head_count = q_heads.shape[1] // HD
    q_rot = rotate(
        q_heads.reshape(seq_rows, head_count, HD).astype(jnp.float32), cos_table, sin_table
    ).astype(jnp.bfloat16)
    k_rot = (
        rotate(k_head.reshape(seq_rows, 1, HD).astype(jnp.float32), cos_table, sin_table)
        .reshape(seq_rows, HD)
        .astype(jnp.bfloat16)
    )
    block_rows = min(512, seq_rows)
    block_count = seq_rows // block_rows
    q_blocks = q_rot.reshape(block_count, block_rows, head_count, HD)
    g_blocks = g_heads.reshape(block_count, block_rows, head_count, HD)
    key_pos = jnp.arange(seq_rows, dtype=jnp.int32)

    def step_block(carry, inputs):
        dk_acc, dv_acc, sink_acc = carry
        q_block, g_block, item_index = inputs
        query_pos = item_index * block_rows + jnp.arange(block_rows, dtype=jnp.int32)
        causal = query_pos[:, None] >= key_pos[None, :]
        scores = SCORE_SCALE * jnp.einsum(
            "qhd,kd->hqk", q_block, k_rot, preferred_element_type=jnp.float32
        )
        scores = jnp.where(causal[None], scores, -jnp.inf)
        row_top = jnp.maximum(jnp.max(scores, axis=-1), sink_here[:, None])
        expd = jnp.exp(scores - row_top[..., None])
        sink_term = jnp.exp(sink_here[:, None] - row_top)
        total = jnp.sum(expd, axis=-1) + sink_term
        prob_f = expd / total[..., None]
        prob_b = prob_f.astype(jnp.bfloat16)
        out_block = jnp.einsum(
            "hqk,kd->qhd", prob_b, v_head, preferred_element_type=jnp.float32
        ).astype(jnp.bfloat16)
        d_prob = jnp.einsum("qhd,kd->hqk", g_block, v_head, preferred_element_type=jnp.float32)
        delta = jnp.sum(prob_f * d_prob, axis=-1)
        d_score = (prob_f * (d_prob - delta[..., None])).astype(jnp.bfloat16)
        dq_rot = SCORE_SCALE * jnp.einsum(
            "hqk,kd->qhd", d_score, k_rot, preferred_element_type=jnp.float32
        )
        cos_block = lax.dynamic_slice_in_dim(cos_table, item_index * block_rows, block_rows, 0)
        sin_block = lax.dynamic_slice_in_dim(sin_table, item_index * block_rows, block_rows, 0)
        dq_block = unrotate(dq_rot, cos_block, sin_block).astype(jnp.bfloat16)
        dk_acc = dk_acc + SCORE_SCALE * jnp.einsum(
            "hqk,qhd->kd", d_score, q_block, preferred_element_type=jnp.float32
        )
        dv_acc = dv_acc + jnp.einsum(
            "hqk,qhd->kd", prob_b, g_block, preferred_element_type=jnp.float32
        )
        sink_acc = sink_acc - jnp.sum(sink_term / total * delta, axis=1)
        return ((dk_acc, dv_acc, sink_acc), (out_block, dq_block))

    start_carry = (
        jnp.zeros((seq_rows, HD), jnp.float32),
        jnp.zeros((seq_rows, HD), jnp.float32),
        jnp.zeros((head_count,), jnp.float32),
    )
    (dk_acc, dv_acc, sink_acc), (out_blocks, dq_blocks) = lax.scan(
        step_block, start_carry, (q_blocks, g_blocks, jnp.arange(block_count, dtype=jnp.int32))
    )
    dk_part = (
        unrotate(dk_acc.reshape(seq_rows, 1, HD), cos_table, sin_table)
        .reshape(seq_rows, HD)
        .astype(jnp.bfloat16)
    )
    dv_part = dv_acc.astype(jnp.bfloat16)
    out_heads = out_blocks.reshape(seq_rows, head_count * HD)
    dq_heads = dq_blocks.reshape(seq_rows, head_count * HD)
    return (out_heads, dq_heads, dk_part, dv_part, sink_acc)


def body(
    query,
    keys,
    values,
    sinks,
    attn_grad,
    moe_in,
    moe_grad,
    expert_ids,
    route_weights,
    w_gate_up,
    w_down,
):
    seq_count = lax.axis_size("seq")
    tok_rows = query.shape[1]
    seq_rows = tok_rows * seq_count
    heads_here = HQ // seq_count
    repeats = seq_count // HK
    my_seq = lax.axis_index("seq")
    cos_table, sin_table = rotary_tables(seq_rows)
    q_local = query.reshape(tok_rows, HQ * HD)
    g_local = attn_grad.reshape(tok_rows, HQ * HD)
    k_local = keys.reshape(tok_rows, HK * HD)
    v_local = values.reshape(tok_rows, HK * HD)
    sink_here = lax.dynamic_slice_in_dim(sinks, my_seq * heads_here, heads_here)
    kv_owner = my_seq // repeats
    q_heads, g_heads = (
        lax.all_to_all(q_local, "seq", split_axis=1, concat_axis=0, tiled=True),
        lax.all_to_all(g_local, "seq", split_axis=1, concat_axis=0, tiled=True),
    )
    k_every, v_every = (
        lax.all_gather(k_local, "seq", axis=0, tiled=True),
        lax.all_gather(v_local, "seq", axis=0, tiled=True),
    )
    k_head = lax.dynamic_slice_in_dim(k_every, kv_owner * HD, HD, 1)
    v_head = lax.dynamic_slice_in_dim(v_every, kv_owner * HD, HD, 1)
    out_heads, dq_heads, dk_part, dv_part, sink_acc = attention_here(
        q_heads, k_head, v_head, g_heads, sink_here, cos_table, sin_table
    )
    out_back, dq_back = (
        lax.all_to_all(out_heads, "seq", split_axis=0, concat_axis=1, tiled=True),
        lax.all_to_all(dq_heads, "seq", split_axis=0, concat_axis=1, tiled=True),
    )
    owner_mask = (jnp.arange(HK, dtype=jnp.int32) == kv_owner)[None, :, None]
    dk_full = jnp.where(owner_mask, dk_part.astype(jnp.float32)[:, None, :], 0.0).reshape(
        seq_rows, HK * HD
    )
    dv_full = jnp.where(owner_mask, dv_part.astype(jnp.float32)[:, None, :], 0.0).reshape(
        seq_rows, HK * HD
    )
    dk_sum, dv_sum = (
        lax.psum_scatter(
            dk_full.astype(jnp.bfloat16), "seq", scatter_dimension=0, tiled=True
        ).astype(jnp.float32),
        lax.psum_scatter(
            dv_full.astype(jnp.bfloat16), "seq", scatter_dimension=0, tiled=True
        ).astype(jnp.float32),
    )
    dk_local = dk_sum.astype(jnp.bfloat16)
    dv_local = dv_sum.astype(jnp.bfloat16)
    head_slots = jnp.arange(HQ, dtype=jnp.int32)
    my_heads = my_seq * heads_here + jnp.arange(heads_here, dtype=jnp.int32)
    sink_vector = jnp.sum(
        jnp.where(head_slots[None, :] == my_heads[:, None], sink_acc[:, None], 0.0), axis=0
    )
    exp_count = lax.axis_size("exp")
    local_experts = w_gate_up.shape[0]
    experts_all = local_experts * exp_count
    x_local = moe_in.reshape(tok_rows, D)
    dy_local = moe_grad.reshape(tok_rows, D)
    route_ids = expert_ids.reshape(tok_rows, TOP)
    route_share = route_weights.reshape(tok_rows, TOP)
    matches = route_ids[:, :, None] == jnp.arange(experts_all, dtype=jnp.int32)[None, None, :]
    hit_table = jnp.any(matches, axis=1)
    token_share = jnp.sum(jnp.where(matches, route_share[:, :, None], 0.0), axis=1)
    slot_rank = jnp.cumsum(hit_table.astype(jnp.int32), axis=0) - 1
    slot_index = jnp.arange(CAP, dtype=jnp.int32)
    chosen = hit_table.T[:, None, :] & (slot_rank.T[:, None, :] == slot_index[None, :, None])
    select_rows = chosen.reshape(experts_all * CAP, tok_rows).astype(jnp.bfloat16)
    weighted_rows = jnp.where(chosen, token_share.T[:, None, :], 0.0).reshape(
        experts_all * CAP, tok_rows
    )
    slot_share = jnp.sum(weighted_rows, axis=1)
    x_send = jnp.dot(select_rows, x_local, preferred_element_type=jnp.float32).astype(jnp.bfloat16)
    dy_send = (
        jnp.dot(select_rows, dy_local, preferred_element_type=jnp.float32) * slot_share[:, None]
    ).astype(jnp.bfloat16)
    x_send = x_send.reshape(exp_count, local_experts, CAP, D)
    dy_send = dy_send.reshape(exp_count, local_experts, CAP, D)
    x_recv, dy_recv = (
        lax.all_to_all(x_send, "exp", split_axis=0, concat_axis=0, tiled=True),
        lax.all_to_all(dy_send, "exp", split_axis=0, concat_axis=0, tiled=True),
    )
    x_rows, dy_rows = (
        lax.all_gather(x_recv, "seq", axis=0, tiled=True),
        lax.all_gather(dy_recv, "seq", axis=0, tiled=True),
    )
    both_proj = jnp.einsum(
        "sjcd,jdtf->sjctf", x_rows, w_gate_up, preferred_element_type=jnp.float32
    )
    gate_part = both_proj[..., 0, :]
    up_part = both_proj[..., 1, :]
    sigmoid_gate = jax.nn.sigmoid(SWIGLU_ALPHA * gate_part)
    hidden = (gate_part * sigmoid_gate * (up_part + 1.0)).astype(jnp.bfloat16)
    d_hidden = jnp.einsum("sjcd,jfd->sjcf", dy_rows, w_down, preferred_element_type=jnp.float32)
    d_gate = (
        d_hidden
        * sigmoid_gate
        * (up_part + 1.0)
        * (1.0 + SWIGLU_ALPHA * gate_part * (1.0 - sigmoid_gate))
    )
    d_up = d_hidden * gate_part * sigmoid_gate
    d_both = jnp.stack([d_gate, d_up], axis=-2).astype(jnp.bfloat16)
    y_own = lax.psum_scatter(
        jnp.einsum("sjcf,jfd->sjcd", hidden, w_down, preferred_element_type=jnp.float32).astype(
            jnp.bfloat16
        ),
        "seq",
        scatter_dimension=0,
        tiled=True,
    )
    dx_own = lax.psum_scatter(
        jnp.einsum(
            "sjctf,jdtf->sjcd", d_both, w_gate_up, preferred_element_type=jnp.float32
        ).astype(jnp.bfloat16),
        "seq",
        scatter_dimension=0,
        tiled=True,
    )
    y_back, dx_back = (
        lax.all_to_all(y_own, "exp", split_axis=0, concat_axis=0, tiled=True),
        lax.all_to_all(dx_own, "exp", split_axis=0, concat_axis=0, tiled=True),
    )
    y_flat = y_back.reshape(experts_all * CAP, D).astype(jnp.float32)
    moe_local = jnp.dot(weighted_rows.T, y_flat, precision=lax.Precision.HIGHEST)
    dx_local = jnp.dot(
        select_rows.T, dx_back.reshape(experts_all * CAP, D), preferred_element_type=jnp.float32
    )
    d_gate_up_part = jnp.einsum(
        "sjcd,sjctf->jdtf", x_rows, d_both, preferred_element_type=jnp.float32
    )
    d_down_part = jnp.einsum("sjcf,sjcd->jfd", hidden, dy_rows, preferred_element_type=jnp.float32)
    d_gate_up_sum, d_down_sum = (
        lax.psum(d_gate_up_part.astype(jnp.bfloat16), "dp").astype(jnp.float32),
        lax.psum(d_down_part.astype(jnp.bfloat16), "dp").astype(jnp.float32),
    )
    d_sinks = lax.psum(sink_vector, ("dp", "seq", "exp"))
    attn_out = out_back.reshape(1, tok_rows, HQ * HD)
    d_query = dq_back.reshape(1, tok_rows, HQ * HD)
    d_keys = dk_local.reshape(1, tok_rows, HK * HD)
    d_values = dv_local.reshape(1, tok_rows, HK * HD)
    moe_out = moe_local.astype(jnp.bfloat16).reshape(1, tok_rows, D)
    d_moe_in = dx_local.astype(jnp.bfloat16).reshape(1, tok_rows, D)
    d_gate_up = d_gate_up_sum.astype(jnp.bfloat16)
    d_down = d_down_sum.astype(jnp.bfloat16)
    return (attn_out, d_query, d_keys, d_values, d_sinks, moe_out, d_moe_in, d_gate_up, d_down)


def solution(mesh):
    return jax.shard_map(
        body,
        mesh=mesh,
        in_specs=(
            P(("dp", "exp"), "seq", None),
            P(("dp", "exp"), "seq", None),
            P(("dp", "exp"), "seq", None),
            P(),
            P(("dp", "exp"), "seq", None),
            P(("dp", "exp"), "seq", None),
            P(("dp", "exp"), "seq", None),
            P(("dp", "exp"), "seq", None),
            P(("dp", "exp"), "seq", None),
            P("exp", None, None, "seq"),
            P("exp", "seq", None),
        ),
        out_specs=(
            P(("dp", "exp"), "seq", None),
            P(("dp", "exp"), "seq", None),
            P(("dp", "exp"), "seq", None),
            P(("dp", "exp"), "seq", None),
            P(),
            P(("dp", "exp"), "seq", None),
            P(("dp", "exp"), "seq", None),
            P("exp", None, None, "seq"),
            P("exp", "seq", None),
        ),
        check_vma=False,
    )
```

profile of v0, /device:TPU:32, one launch (start us, length us, event | category | flops | bytes accessed | tf_op | source)
XLA Modules:
  0.0 600.9 jit_solution(15439015337323017819)
XLA Ops:
  13.1 17.3 %all_to_all.81 = bf16[8,1,4,2880]{3,2,1,0:T(4,128)(2,1)} all-to-all(bf16[8,1,4,2880]{3,2,1,0:T(4,128)(2,1)S(1)} %bitcast.387), channel_id=1, replica_groups=mesh['dp'=2,'seq'=16,'exp'=8] {'exp'}, dimensions={0} | all-to-all | bytes 368640 | tf_op jit(solution)/shard_map/all_to_all | solution.py:230
  32.1 12.7 %all_to_all.82 = bf16[8,1,4,2880]{3,2,1,0:T(4,128)(2,1)} all-to-all(bf16[8,1,4,2880]{3,2,1,0:T(4,128)(2,1)S(1)} %bitcast.388), channel_id=1, replica_groups=mesh['dp'=2,'seq'=16,'exp'=8] {'exp'}, dimensions={0} | all-to-all | bytes 368640 | tf_op jit(solution)/shard_map/all_to_all | solution.py:231
  45.9 7.0 %all-to-all-start = ((bf16[128,16,128]{0,2,1:T(8,128)(2,1)}), bf16[128,16,128]{0,2,1:T(8,128)(2,1)S(1)}, u32[]{:S(2)}, u32[]{:S(2)}) async-start(bf16[128,16,128]{0,2,1:T(8,128)(2,1)} %bitcast), calls=%async_computation | async-start | bytes 1048576 | tf_op jit(solution)/shard_map/all_to_all | solution.py:167
  55.8 8.3 %all-to-all-done = bf16[128,16,128]{0,2,1:T(8,128)(2,1)S(1)} async-done(((bf16[128,16,128]{0,2,1:T(8,128)(2,1)}), bf16[128,16,128]{0,2,1:T(8,128)(2,1)S(1)}, u32[]{:S(2)}, u32[]{:S(2)}) %all-to-all-start) | async-done | bytes 524320 | tf_op jit(solution)/shard_map/all_to_all | solution.py:167
  64.2 4.2 all-to-all-start.1
  69.0 1.6 copy.156
  74.6 3.9 all-to-all-done.1
  80.9 1.9 copy.162
  84.3 29.0 %all-gather.11.cloned.1.call-done = bf16[1,2048,256]{1,2,0:T(8,128)(2,1)} async-done(((bf16[1,128,256]{1,2,0:T(8,128)(2,1)}), bf16[1,2048,256]{1,2,0:T(8,128)(2,1)}) %all-gather.11.cloned.1.call-update) | async-done | bytes 1048592 | tf_op jit(solution)/shard_map/all_gather | solution.py:171
  115.5 52.2 %all-gather.7.cloned.1.call-done = bf16[128,1,4,2880]{3,2,1,0:T(4,128)(2,1)} async-done(((bf16[8,1,4,2880]{3,2,1,0:T(4,128)(2,1)}), bf16[128,1,4,2880]{3,2,1,0:T(4,128)(2,1)}) %all-gather.7.cloned.1.call-update) | async-done | bytes 2949136 | tf_op jit(solution)/shard_map/all_gather | solution.py:234
  167.7 6.1 %copy.170 = bf16[128,1,4,2880]{0,3,2,1:T(8,128)(2,1)} copy(bf16[128,1,4,2880]{3,2,1,0:T(4,128)(2,1)} %all-gather.7.cloned.1.call-done) | data formatting | bytes 5898240 | tf_op jit(solution)/shard_map/all_gather | solution.py:234
  173.8 3.8 fusion.68
  178.5 2.7 fusion.50
  181.2 40.5 %all-gather.9.cloned.1.call-done = bf16[128,1,4,2880]{3,2,1,0:T(4,128)(2,1)} async-done(((bf16[8,1,4,2880]{3,2,1,0:T(4,128)(2,1)}), bf16[128,1,4,2880]{3,2,1,0:T(4,128)(2,1)}) %all-gather.9.cloned.1.call-update) | async-done | bytes 2949136 | tf_op jit(solution)/shard_map/all_gather | solution.py:235
  221.7 6.1 %copy.179 = bf16[128,1,4,2880]{0,3,2,1:T(8,128)(2,1)} copy(bf16[128,1,4,2880]{3,2,1,0:T(4,128)(2,1)} %all-gather.9.cloned.1.call-done) | data formatting | bytes 5898240 | tf_op jit(solution)/shard_map/all_gather | solution.py:235
  227.8 3.0 fusion.104
  231.5 3.3 fusion.49
  234.8 6.2 %copy.181 = bf16[128,1,4,2880]{3,2,1,0:T(4,128)(2,1)} copy(bf16[128,1,4,2880]{0,3,2,1:T(8,128)(2,1)} %fusion.49) | data formatting | bytes 5898240 | tf_op jit(solution)/shard_map/convert_element_type | solution.py:264
  241.0 6.2 %copy.175 = bf16[128,1,4,2880]{3,2,1,0:T(4,128)(2,1)} copy(bf16[128,1,4,2880]{0,3,2,1:T(8,128)(2,1)} %fusion.50) | data formatting | bytes 5898240 | tf_op jit(solution)/shard_map/convert_element_type | solution.py:254
  247.3 133.2 %while.19 = (s32[]{:T(128)}, f32[2048,64]{0,1:T(8,128)S(1)}, f32[2048,64]{0,1:T(8,128)}, f32[2]{0:T(128)S(1)}, bf16[4,512,2,64]{1,3,2,0:T(8,128)(2,1)}, /*index=...) while((s32[]{:T(128)}, f32[2048,64]{0,1:T(8,128)S(1)}, ...), condition=%wide.region_5.6_spmd.clone, body=%wide.region_0.5_spmd.clone.sunk | while | flops 1675894272 | bytes 159345072 | solution.py:126
  249.4 1.8 bitcast_reduce_fusion.2
  251.3 2.5 fusion.160
  253.9 4.4 fusion.162
  258.3 2.9 fusion.163
  261.2 2.0 copy-done.2
  265.4 7.0 %fusion.167 = bf16[4,512,2,64]{1,3,2,0:T(8,128)(2,1)} fusion(bf16[4,512,2,64]{1,3,2,0:T(8,128)(2,1)} %get-tuple-element.443, s32[]{:T(128)} %get-tuple-element.439, bf16[2048,64]{0,1:T(8,128)(2,1)S(1)} %get-tuple-element.468, f32[512,2,2048]{2,0,1:T(8,128)} %copy-done.4, f32[2,512]{1,0:T(2,128)S(1)} %fusion.161, ...), kind=kOutput, calls=%fused_computation.25.clone.1 | convolution fusion | flops 278986752 | bytes 9839104 | tf_op jit(solution)/shard_map/while/body/eval_jaxpr/hqk,kd->qhd/dot_general | solution.py:100
  272.6 7.3 %fusion.165 = f32[2048,64]{0,1:T(8,128)} fusion(f32[2048,64]{0,1:T(8,128)} %get-tuple-element.441, pred[]{:T(512)S(6)} %compare.5, bf16[4,512,2,64]{1,3,2,0:T(8,128)(2,1)} %get-tuple-element.467, s32[]{:T(128)} %get-tuple-element.439, f32[512,2,2048]{2,0,1:T(8,128)} %copy-done.4, f32[2,512]{1,0:T(2,128)S(1)} %fusion.161, ...), kind=kOutput, calls=%fused_computation.14.clone.1 | convolution fusion | flops 279183360 | bytes 10625537 | tf_op jit(solution)/shard_map/while/body/eval_jaxpr/hqk,qhd->kd/dot_general | solution.py:115
  282.7 1.8 bitcast_reduce_fusion.2
  284.6 2.5 fusion.160
  287.2 4.4 fusion.162
  291.6 2.9 fusion.163
  294.6 2.0 copy-done.2
  298.7 6.8 %fusion.167 = bf16[4,512,2,64]{1,3,2,0:T(8,128)(2,1)} fusion(bf16[4,512,2,64]{1,3,2,0:T(8,128)(2,1)} %get-tuple-element.443, s32[]{:T(128)} %get-tuple-element.439, bf16[2048,64]{0,1:T(8,128)(2,1)S(1)} %get-tuple-element.468, f32[512,2,2048]{2,0,1:T(8,128)} %copy-done.4, f32[2,512]{1,0:T(2,128)S(1)} %fusion.161, ...), kind=kOutput, calls=%fused_computation.25.clone.1 | convolution fusion | flops 278986752 | bytes 9839104 | tf_op jit(solution)/shard_map/while/body/eval_jaxpr/hqk,kd->qhd/dot_general | solution.py:100
  305.7 7.3 %fusion.165 = f32[2048,64]{0,1:T(8,128)} fusion(f32[2048,64]{0,1:T(8,128)} %get-tuple-element.441, pred[]{:T(512)S(6)} %compare.5, bf16[4,512,2,64]{1,3,2,0:T(8,128)(2,1)} %get-tuple-element.467, s32[]{:T(128)} %get-tuple-element.439, f32[512,2,2048]{2,0,1:T(8,128)} %copy-done.4, f32[2,512]{1,0:T(2,128)S(1)} %fusion.161, ...), kind=kOutput, calls=%fused_computation.14.clone.1 | convolution fusion | flops 279183360 | bytes 10625537 | tf_op jit(solution)/shard_map/while/body/eval_jaxpr/hqk,qhd->kd/dot_general | solution.py:115
  315.8 1.8 bitcast_reduce_fusion.2
  317.7 2.5 fusion.160
  320.3 4.4 fusion.162
  324.8 2.9 fusion.163
  327.7 2.0 copy-done.2
  331.8 6.8 %fusion.167 = bf16[4,512,2,64]{1,3,2,0:T(8,128)(2,1)} fusion(bf16[4,512,2,64]{1,3,2,0:T(8,128)(2,1)} %get-tuple-element.443, s32[]{:T(128)} %get-tuple-element.439, bf16[2048,64]{0,1:T(8,128)(2,1)S(1)} %get-tuple-element.468, f32[512,2,2048]{2,0,1:T(8,128)} %copy-done.4, f32[2,512]{1,0:T(2,128)S(1)} %fusion.161, ...), kind=kOutput, calls=%fused_computation.25.clone.1 | convolution fusion | flops 278986752 | bytes 9839104 | tf_op jit(solution)/shard_map/while/body/eval_jaxpr/hqk,kd->qhd/dot_general | solution.py:100
  338.9 7.2 %fusion.165 = f32[2048,64]{0,1:T(8,128)} fusion(f32[2048,64]{0,1:T(8,128)} %get-tuple-element.441, pred[]{:T(512)S(6)} %compare.5, bf16[4,512,2,64]{1,3,2,0:T(8,128)(2,1)} %get-tuple-element.467, s32[]{:T(128)} %get-tuple-element.439, f32[512,2,2048]{2,0,1:T(8,128)} %copy-done.4, f32[2,512]{1,0:T(2,128)S(1)} %fusion.161, ...), kind=kOutput, calls=%fused_computation.14.clone.1 | convolution fusion | flops 279183360 | bytes 10625537 | tf_op jit(solution)/shard_map/while/body/eval_jaxpr/hqk,qhd->kd/dot_general | solution.py:115
  348.9 1.8 bitcast_reduce_fusion.2
  350.8 2.5 fusion.160
  353.4 4.4 fusion.162
  357.9 2.9 fusion.163
  360.8 2.0 copy-done.2
  364.9 7.0 %fusion.167 = bf16[4,512,2,64]{1,3,2,0:T(8,128)(2,1)} fusion(bf16[4,512,2,64]{1,3,2,0:T(8,128)(2,1)} %get-tuple-element.443, s32[]{:T(128)} %get-tuple-element.439, bf16[2048,64]{0,1:T(8,128)(2,1)S(1)} %get-tuple-element.468, f32[512,2,2048]{2,0,1:T(8,128)} %copy-done.4, f32[2,512]{1,0:T(2,128)S(1)} %fusion.161, ...), kind=kOutput, calls=%fused_computation.25.clone.1 | convolution fusion | flops 278986752 | bytes 9839104 | tf_op jit(solution)/shard_map/while/body/eval_jaxpr/hqk,kd->qhd/dot_general | solution.py:100
  372.1 7.2 %fusion.165 = f32[2048,64]{0,1:T(8,128)} fusion(f32[2048,64]{0,1:T(8,128)} %get-tuple-element.441, pred[]{:T(512)S(6)} %compare.5, bf16[4,512,2,64]{1,3,2,0:T(8,128)(2,1)} %get-tuple-element.467, s32[]{:T(128)} %get-tuple-element.439, f32[512,2,2048]{2,0,1:T(8,128)} %copy-done.4, f32[2,512]{1,0:T(2,128)S(1)} %fusion.161, ...), kind=kOutput, calls=%fused_computation.14.clone.1 | convolution fusion | flops 279183360 | bytes 10625537 | tf_op jit(solution)/shard_map/while/body/eval_jaxpr/hqk,qhd->kd/dot_general | solution.py:115
  386.1 4.1 fusion.53
  390.2 2.8 fusion.51
  394.6 4.5 all-to-all-start.2
  400.7 10.2 %all-to-all-done.2 = bf16[16,128,128]{1,2,0:T(8,128)(2,1)S(1)} async-done(((bf16[16,128,128]{1,2,0:T(8,128)(2,1)}), bf16[16,128,128]{1,2,0:T(8,128)(2,1)S(1)}, u32[]{:S(2)}, u32[]{:S(2)}) %all-to-all-start.2) | async-done | bytes 524320 | tf_op jit(solution)/shard_map/all_to_all | solution.py:180
  410.9 3.6 all-to-all-start.3
  415.9 1.7 constant_dynamic-slice_fusion.2
  417.5 7.8 %all-to-all-done.3 = bf16[16,128,128]{1,2,0:T(8,128)(2,1)S(1)} async-done(((bf16[16,128,128]{1,2,0:T(8,128)(2,1)}), bf16[16,128,128]{1,2,0:T(8,128)(2,1)S(1)}, u32[]{:S(2)}, u32[]{:S(2)}) %all-to-all-start.3) | async-done | bytes 524320 | tf_op jit(solution)/shard_map/all_to_all | solution.py:181
  425.3 7.4 %all-to-all-start.7 = ((bf16[8,1,4,2880]{3,2,1,0:T(4,128)(2,1)}), bf16[8,1,4,2880]{3,2,1,0:T(4,128)(2,1)S(1)}, u32[]{:S(2)}, u32[]{:S(2)}) async-start(bf16[8,1,4,2880]{3,2,1,0:T(4,128)(2,1)} %constant_dynamic-slice_fusion.2), calls=%async_computation.7 | async-start | bytes 376832 | tf_op jit(solution)/shard_map/all_to_all | solution.py:271
  432.7 1.7 constant_dynamic-slice_fusion.3
  434.4 6.5 %all-to-all-done.7 = bf16[8,1,4,2880]{3,2,1,0:T(4,128)(2,1)S(1)} async-done(((bf16[8,1,4,2880]{3,2,1,0:T(4,128)(2,1)}), bf16[8,1,4,2880]{3,2,1,0:T(4,128)(2,1)S(1)}, u32[]{:S(2)}, u32[]{:S(2)}) %all-to-all-start.7) | async-done | bytes 184352 | tf_op jit(solution)/shard_map/all_to_all | solution.py:271
  440.9 4.8 all-to-all-start.5
  445.7 73.8 %psum.21 = f32[32]{0:T(128)} all-reduce(f32[32]{0:T(128)S(1)} %fusion.110), channel_id=1, replica_groups=mesh['dp'=2,'seq'=16,'exp'=8] {'dp','seq','exp'}, use_global_device_ids=true, to_apply=%region_9.10 | all-reduce | flops 32 | bytes 256 | tf_op jit(solution)/shard_map/psum | solution.py:286
  523.3 24.5 %reduce-scatter.9.cloned.1.call-done = bf16[128,256]{1,0:T(8,128)(2,1)} async-done(((bf16[2048,256]{1,0:T(8,128)(2,1)}), bf16[128,256]{1,0:T(8,128)(2,1)}) %reduce-scatter.9.cloned.1.call-update) | async-done | bytes 65552
  549.4 35.5 %all-reduce.9.cloned.1.call-done = (bf16[1,2880,2,180]{1,3,2,0:T(8,128)(2,1)}, bf16[1,180,2880]{2,1,0:T(8,128)(2,1)}) async-done(((bf16[1,2880,2,180]{1,3,2,0:T(8,128)(2,1)}, bf16[1,180,2880]{2,1,0:T(8,128)(2,1)}), (bf16[1,2880,2,180]{1,3,2,0:T(8,128)(2,1)}, bf16[1,180,2880]{2,1,0:T(8,128)(2,1)})) %all-reduce.9.cloned.1.call-update) | async-done | bytes 3110416 | tf_op jit(solution)/shard_map/psum | solution.py:283
  584.9 4.7 copy.186
  591.1 1.8 fusion.54
  (204 shorter events, 59.4 us)
Async XLA Ops:
  7.2 171.3 %copy-start = (bf16[1,180,2880]{2,1,0:T(8,128)(2,1)S(1)}, bf16[1,180,2880]{2,1,0:T(8,128)(2,1)}, u32[]{:S(2)}) copy-start(bf16[1,180,2880]{2,1,0:T(8,128)(2,1)} %param.23) | copy-start | bytes 3110404
  7.2 37.6 %copy-start.7 = (bf16[1,128,2048]{2,1,0:T(8,128)(2,1)S(1)}, bf16[1,128,2048]{2,1,0:T(8,128)(2,1)}, u32[]{:S(2)}) copy-start(bf16[1,128,2048]{2,1,0:T(8,128)(2,1)} %param.13) | copy-start | bytes 1572868
  7.2 45.8 %copy-start.8 = (bf16[1,128,2048]{2,1,0:T(8,128)(2,1)S(1)}, bf16[1,128,2048]{2,1,0:T(8,128)(2,1)}, u32[]{:S(2)}) copy-start(bf16[1,128,2048]{2,1,0:T(8,128)(2,1)} %param.17) | copy-start | bytes 1572868
  7.2 47.5 %copy-start.21 = (f32[32]{0:T(128)S(1)}, f32[32]{0:T(128)}, u32[]{:S(2)}) copy-start(f32[32]{0:T(128)} %param.16) | copy-start | bytes 388
  7.2 75.6 %all-gather.13.cloned.1.call-start = ((), (), s32[]{:S(2)}) async-start(), calls=%async_computation.13 | async-start | bytes 1114112 | tf_op jit(solution)/shard_map/all_gather | solution.py:172
  8.0 105.3 %all-gather.11.cloned.1.call-start = ((), (), s32[]{:S(2)}) async-start(), calls=%async_computation.12 | async-start | bytes 1114112 | tf_op jit(solution)/shard_map/all_gather | solution.py:171
  9.6 158.1 %all-gather.7.cloned.1.call-start = ((), (), s32[]{:S(2)}) async-start(), calls=%async_computation.10 | async-start | bytes 3203072 | tf_op jit(solution)/shard_map/all_gather | solution.py:234
  11.4 34.4 %copy-start.15 = (f32[128,8]{0,1:T(8,128)}, f32[128,8]{0,1:T(8,128)S(1)}, u32[]{:S(2)}) copy-start(f32[128,8]{0,1:T(8,128)S(1)} %select_reduce_fusion) | copy-start | bytes 12292
  11.5 34.3 %copy-start.13 = (pred[8,4,128]{2,1,0:T(4,128)(4,1)}, pred[8,4,128]{2,1,0:T(4,128)(4,1)S(1)}, u32[]{:S(2)}) copy-start(pred[8,4,128]{2,1,0:T(4,128)(4,1)S(1)} %get-tuple-element.299) | copy-start | bytes 12292
  30.4 191.3 %all-gather.9.cloned.1.call-start = ((), (), s32[]{:S(2)}) async-start(), calls=%async_computation.11 | async-start | bytes 3203072 | tf_op jit(solution)/shard_map/all_gather | solution.py:235
  45.9 18.3 %all-to-all-start = ((bf16[128,16,128]{0,2,1:T(8,128)(2,1)}), bf16[128,16,128]{0,2,1:T(8,128)(2,1)S(1)}, u32[]{:S(2)}, u32[]{:S(2)}) async-start(bf16[128,16,128]{0,2,1:T(8,128)(2,1)} %bitcast), calls=%async_computation | async-start | bytes 1048576 | tf_op jit(solution)/shard_map/all_to_all | solution.py:167
  52.9 61.4 %copy-start.17 = (f32[32]{0:T(128)}, f32[32]{0:T(128)S(1)}, u32[]{:S(2)}) copy-start(f32[32]{0:T(128)S(1)} %multiply_add_fusion) | copy-start | bytes 388
  64.2 14.4 %all-to-all-start.1 = ((bf16[128,16,128]{0,2,1:T(8,128)(2,1)}), bf16[128,16,128]{0,2,1:T(8,128)(2,1)}, u32[]{:S(2)}, u32[]{:S(2)}) async-start(bf16[128,16,128]{0,2,1:T(8,128)(2,1)} %bitcast.5), calls=%async_computation.1 | async-start | bytes 1048576 | tf_op jit(solution)/shard_map/all_to_all | solution.py:168
  68.4 347.4 %all-reduce.7.cloned.1.call-start = ((), (), s32[]{:S(2)}) async-start(), calls=%async_computation.16 | async-start | bytes 12058624
  177.6 0.9 copy-start.11
  227.8 3.7 copy-start.20
  230.8 0.7 copy-start.25
  230.8 10.2 %copy-start.23 = (bf16[128,4,1,180]{0,3,1,2:T(8,128)(2,1)}, bf16[128,4,1,180]{0,3,1,2:T(8,128)(2,1)S(1)}, u32[]{:S(2)}) copy-start(bf16[128,4,1,180]{0,3,1,2:T(8,128)(2,1)S(1)} %get-tuple-element.310) | copy-start | bytes 552964
  247.2 274.4 %reduce-scatter.7.cloned.1.call-start = ((), (), s32[]{:S(2)}) async-start(), calls=%async_computation.14 | async-start | bytes 1114112
  247.2 134.3 %copy-start.18 = (f32[32]{0:T(128)S(1)}, f32[32]{0:T(128)}, u32[]{:S(2)}) copy-start(f32[32]{0:T(128)} %copy-done.17) | copy-start | bytes 388
  247.3 135.5 %copy-start.19 = (pred[256]{0:T(512)(128)(4,1)S(1)}, pred[256]{0:T(512)(128)(4,1)}, u32[]{:S(2)}) copy-start(pred[256]{0:T(512)(128)(4,1)} %broadcast_in_dim.123) | copy-start | bytes 772
  251.2 7.1 %copy-start.4 = (f32[512,2,2048]{2,0,1:T(8,128)}, f32[512,2,2048]{2,0,1:T(8,128)S(1)}, u32[]{:S(2)}) copy-start(f32[512,2,2048]{2,0,1:T(8,128)S(1)} %get-tuple-element.413) | copy-start | bytes 25165828 | tf_op jit(solution)/shard_map/while
  261.2 2.0 copy-start.2
  272.6 7.3 %copy-start.3 = (bf16[2,512,2048]{2,1,0:T(8,128)(2,1)S(1)}, bf16[2,512,2048]{2,1,0:T(8,128)(2,1)}, u32[]{:S(2)}) copy-start(bf16[2,512,2048]{2,1,0:T(8,128)(2,1)} %copy-done.2) | copy-start | bytes 12582916 | tf_op jit(solution)/shard_map/while
  284.5 7.1 %copy-start.4 = (f32[512,2,2048]{2,0,1:T(8,128)}, f32[512,2,2048]{2,0,1:T(8,128)S(1)}, u32[]{:S(2)}) copy-start(f32[512,2,2048]{2,0,1:T(8,128)S(1)} %get-tuple-element.413) | copy-start | bytes 25165828 | tf_op jit(solution)/shard_map/while
  294.5 2.0 copy-start.2
  305.7 7.3 %copy-start.3 = (bf16[2,512,2048]{2,1,0:T(8,128)(2,1)S(1)}, bf16[2,512,2048]{2,1,0:T(8,128)(2,1)}, u32[]{:S(2)}) copy-start(bf16[2,512,2048]{2,1,0:T(8,128)(2,1)} %copy-done.2) | copy-start | bytes 12582916 | tf_op jit(solution)/shard_map/while
  317.6 7.1 %copy-start.4 = (f32[512,2,2048]{2,0,1:T(8,128)}, f32[512,2,2048]{2,0,1:T(8,128)S(1)}, u32[]{:S(2)}) copy-start(f32[512,2,2048]{2,0,1:T(8,128)S(1)} %get-tuple-element.413) | copy-start | bytes 25165828 | tf_op jit(solution)/shard_map/while
  327.7 2.0 copy-start.2
  338.9 7.2 %copy-start.3 = (bf16[2,512,2048]{2,1,0:T(8,128)(2,1)S(1)}, bf16[2,512,2048]{2,1,0:T(8,128)(2,1)}, u32[]{:S(2)}) copy-start(bf16[2,512,2048]{2,1,0:T(8,128)(2,1)} %copy-done.2) | copy-start | bytes 12582916 | tf_op jit(solution)/shard_map/while
  350.8 7.1 %copy-start.4 = (f32[512,2,2048]{2,0,1:T(8,128)}, f32[512,2,2048]{2,0,1:T(8,128)S(1)}, u32[]{:S(2)}) copy-start(f32[512,2,2048]{2,0,1:T(8,128)S(1)} %get-tuple-element.413) | copy-start | bytes 25165828 | tf_op jit(solution)/shard_map/while
  360.8 2.0 copy-start.2
  372.1 7.2 %copy-start.3 = (bf16[2,512,2048]{2,1,0:T(8,128)(2,1)S(1)}, bf16[2,512,2048]{2,1,0:T(8,128)(2,1)}, u32[]{:S(2)}) copy-start(bf16[2,512,2048]{2,1,0:T(8,128)(2,1)} %copy-done.2) | copy-start | bytes 12582916 | tf_op jit(solution)/shard_map/while
  382.8 3.3 copy-start.12
  384.6 5.6 copy-start.24
  384.6 5.6 copy-start.26
  384.6 163.1 %reduce-scatter.9.cloned.1.call-start = ((), (), s32[]{:S(2)}) async-start(), calls=%async_computation.15 | async-start | bytes 1114112
  386.0 198.9 %all-reduce.9.cloned.1.call-start = ((), (), s32[]{:S(2)}) async-start(), calls=%async_computation.17 | async-start | bytes 6500352 | tf_op jit(solution)/shard_map/psum | solution.py:283
  386.1 4.1 copy-start.5
  390.2 2.8 copy-start.9
  393.0 6.1 %copy-start.10 = (bf16[4,512,2,64]{1,3,2,0:T(8,128)(2,1)S(1)}, bf16[4,512,2,64]{1,3,2,0:T(8,128)(2,1)}, u32[]{:S(2)}) copy-start(bf16[4,512,2,64]{1,3,2,0:T(8,128)(2,1)} %get-tuple-element.91) | copy-start | bytes 1572868
  393.0 21.5 %copy-start.22 = (u32[256]{0:T(256)S(1)}, u32[256]{0:T(256)}, u32[]{:S(2)}) copy-start(u32[256]{0:T(256)} %constant.101) | copy-start | bytes 3076
  393.5 52.3 %copy-start.14 = (pred[8,4,128]{2,1,0:T(4,128)(4,1)S(1)}, pred[8,4,128]{2,1,0:T(4,128)(4,1)}, u32[]{:S(2)}) copy-start(pred[8,4,128]{2,1,0:T(4,128)(4,1)} %copy-done.13) | copy-start | bytes 12292
  393.5 52.3 %copy-start.16 = (f32[128,8]{0,1:T(8,128)S(1)}, f32[128,8]{0,1:T(8,128)}, u32[]{:S(2)}) copy-start(f32[128,8]{0,1:T(8,128)} %copy-done.15) | copy-start | bytes 12292
  394.6 16.3 %all-to-all-start.2 = ((bf16[16,128,128]{1,2,0:T(8,128)(2,1)}), bf16[16,128,128]{1,2,0:T(8,128)(2,1)S(1)}, u32[]{:S(2)}, u32[]{:S(2)}) async-start(bf16[16,128,128]{1,2,0:T(8,128)(2,1)} %copy.164), calls=%async_computation.2 | async-start | bytes 1048576 | tf_op jit(solution)/shard_map/all_to_all | solution.py:180
  410.9 14.4 %all-to-all-start.3 = ((bf16[16,128,128]{1,2,0:T(8,128)(2,1)}), bf16[16,128,128]{1,2,0:T(8,128)(2,1)S(1)}, u32[]{:S(2)}, u32[]{:S(2)}) async-start(bf16[16,128,128]{1,2,0:T(8,128)(2,1)} %copy.166), calls=%async_computation.3 | async-start | bytes 1048576 | tf_op jit(solution)/shard_map/all_to_all | solution.py:181
  425.3 15.6 %all-to-all-start.7 = ((bf16[8,1,4,2880]{3,2,1,0:T(4,128)(2,1)}), bf16[8,1,4,2880]{3,2,1,0:T(4,128)(2,1)S(1)}, u32[]{:S(2)}, u32[]{:S(2)}) async-start(bf16[8,1,4,2880]{3,2,1,0:T(4,128)(2,1)} %constant_dynamic-slice_fusion.2), calls=%async_computation.7 | async-start | bytes 376832 | tf_op jit(solution)/shard_map/all_to_all | solution.py:271
  440.9 150.1 %all-to-all-start.5 = ((bf16[8,1,4,2880]{3,2,1,0:T(4,128)(2,1)}), bf16[8,1,4,2880]{3,2,1,0:T(4,128)(2,1)S(1)}, u32[]{:S(2)}, u32[]{:S(2)}) async-start(bf16[8,1,4,2880]{3,2,1,0:T(4,128)(2,1)} %constant_dynamic-slice_fusion.3), calls=%async_computation.5 | async-start | bytes 376832 | tf_op jit(solution)/shard_map/all_to_all | solution.py:270
  584.9 7.9 %copy-start.6 = (bf16[1,180,2880]{2,1,0:T(8,128)(2,1)S(1)}, bf16[1,180,2880]{2,1,0:T(8,128)(2,1)}, u32[]{:S(2)}) copy-start(bf16[1,180,2880]{2,1,0:T(8,128)(2,1)} %get-tuple-element.483) | copy-start | bytes 3110404
  584.9 8.9 %copy-start.1 = (bf16[1,180,2880]{2,1,0:T(8,128)(2,1)S(1)}, bf16[1,180,2880]{2,1,0:T(8,128)(2,1)}, u32[]{:S(2)}) copy-start(bf16[1,180,2880]{2,1,0:T(8,128)(2,1)} %param.23) | copy-start | bytes 3110404
Sparse Core Ops, SparseCore 0:
  10.5 52.3 all-gather.12
  65.9 47.3 all-gather.10
  115.7 51.9 all-gather.6
  170.0 51.6 all-gather.8
  247.3 129.4 all-reduce.6
  384.7 82.0 reduce-scatter.6
  470.3 77.3 reduce-scatter.8
  551.2 33.6 all-reduce.8
where the time goes:
time: 608 us; the launch traced here: 601 us
  waiting for transfers between devices  219 us (36%)
  matrix products  116 us (19%)
  blocking collectives  104 us (17%)
  local copies, waits for them, and re-layouts  72.3 us (12%)
  other arithmetic  37.7 us (6%)
  starting transfers between devices  32.4 us (5%)
  between operations  15.6 us (3%)
    psum x1, blocking collectives, body(): d_sinks = lax.psum(sink_vector, ('dp', 'seq', 'exp'))  73.8 us
    all_gather x1, waiting for transfers between devices, body(): lax.all_gather(x_recv, 'seq', axis=0, tiled=True)  52.2 us
    all_gather x1, waiting for transfers between devices, body(): lax.all_gather(dy_recv, 'seq', axis=0, tiled=True)  40.5 us
    psum x1, waiting for transfers between devices, body(): lax.psum(d_gate_up_part.astype(jnp.bfloat16), 'dp').astype(jnp.float32)  35.5 us
    all_gather x1, waiting for transfers between devices, body(): lax.all_gather(k_local, 'seq', axis=0, tiled=True)  29 us
    dot_general x4, matrix products, step_block(): jnp.einsum('hqk,qhd->kd', prob_b, g_block, preferred_element_type=jnp.flo...  28.9 us
    dot_general x4, matrix products, step_block(): jnp.einsum('hqk,kd->qhd', prob_b, v_head, preferred_element_type=jnp.floa...  27.5 us
    unnamed x11, waiting for transfers between devices  25.3 us
  transfers between devices with their start and end apart: 14, of which 10 were waited for; matrix products, arithmetic and copies ran while one was open for 31% of the time, Pallas kernels for 0%

commit v1 on v0

v1 whole, which is shorter than its diff:
```python
import math

import jax
import jax.numpy as jnp
from jax import lax
from jax.experimental import pallas as pl
from jax.experimental.pallas import tpu as pltpu
from jax.sharding import PartitionSpec as P

D = 2880
HQ = 32
HK = 4
HD = 64
TOP = 4
CAP = 4
FFD = 180
ROWS = 32

ROPE_BASE = 150000.0
YARN_FACTOR = 32.0
YARN_INITIAL = 4096.0
BETA_FAST = 32.0
BETA_SLOW = 1.0
SWIGLU_ALPHA = 1.702
SCORE_SCALE = 0.125

MESH = pl.DeviceIdType.MESH
F32 = jnp.float32
BF16 = jnp.bfloat16
NT = (((1,), (1,)), ((), ()))
TN = (((0,), (0,)), ((), ()))


def dot(a, b, dims=(((1,), (0,)), ((), ()))):
    return lax.dot_general(a, b, dims, preferred_element_type=F32)


def swap_halves(y, lanes):
    return jnp.where((lanes & 32) == 0, pltpu.roll(y, 96, 1), pltpu.roll(y, 32, 1))


class Comm:
    def __init__(self, send, recv):
        seq = lax.axis_index("seq")
        self.y, self.x = seq // 4, lax.rem(seq, 4)
        self.z = lax.axis_index("exp")
        self.c = lax.axis_index("dp")
        self.send, self.recv, self.used = send, recv, 0
        self.all = []

    def at_x(self, k):
        return {"seq": self.y * 4 + lax.rem(self.x + k, 4)}

    def at_y(self, k):
        return {"seq": lax.rem(self.y + k, 4) * 4 + self.x}

    def at_z(self, k):
        return {"exp": lax.rem(self.z + k, 8)}

    def at_c(self):
        return {"dp": 1 - self.c}

    def copy(self, src, dst, where):
        i = self.used
        self.used += 1
        made = pltpu.make_async_remote_copy(
            src_ref=src,
            dst_ref=dst,
            send_sem=self.send.at[i],
            recv_sem=self.recv.at[i],
            device_id=where,
            device_id_type=MESH,
        )
        self.all.append(made)
        return made


def start(copies):
    for made in copies:
        made.start()


def arrived(copies):
    for made in copies:
        made.wait_recv()


class Gather:
    def __init__(self, comm, buf, x_first):
        self.buf, self.x_first = buf, x_first
        self.rows = buf.shape[2]
        i, j = (comm.y, comm.x) if x_first else (comm.x, comm.y)
        near, far = (comm.at_x, comm.at_y) if x_first else (comm.at_y, comm.at_x)
        h = self.rows // 2
        jl, jr = lax.rem(j + 3, 4), lax.rem(j + 1, 4)
        il, ir = lax.rem(i + 3, 4), lax.rem(i + 1, 4)
        low, high = pl.ds(0, h), pl.ds(h, h)
        b = self.block
        self.steps = [
            [comm.copy(b(i, j), b(i, j), near(1)), comm.copy(b(i, j), b(i, j), near(3))],
            [
                comm.copy(b(i, jl, low), b(i, jl, low), near(1)),
                comm.copy(b(i, jr, high), b(i, jr, high), near(3)),
            ],
            [
                comm.copy(b(i, pl.ds(0, 4)), b(i, pl.ds(0, 4)), far(1)),
                comm.copy(b(i, pl.ds(0, 4)), b(i, pl.ds(0, 4)), far(3)),
            ],
            [
                comm.copy(b(il, pl.ds(0, 2)), b(il, pl.ds(0, 2)), far(1)),
                comm.copy(b(ir, pl.ds(2, 2)), b(ir, pl.ds(2, 2)), far(3)),
            ],
        ]

    def block(self, i, j, rows=None):
        index = (i, j) if self.x_first else (j, i)
        return self.buf.at[index] if rows is None else self.buf.at[index + (rows,)]


class Scatter:
    def __init__(self, comm, buf, y_first, r1, r2, r3, r4):
        self.buf, self.y_first = buf, y_first
        self.rows = buf.shape[2]
        i, j = (comm.y, comm.x) if y_first else (comm.x, comm.y)
        first, second = (comm.at_y, comm.at_x) if y_first else (comm.at_x, comm.at_y)
        self.i, self.j = i, j
        self.r = (r1, r2, r3, r4)
        h = self.rows // 2
        self.i1, self.i2, self.i3 = (lax.rem(i + k, 4) for k in (1, 2, 3))
        self.j1, self.j2, self.j3 = (lax.rem(j + k, 4) for k in (1, 2, 3))
        b = self.block
        self.s1 = [
            comm.copy(b(self.i2, pl.ds(0, 2)), r1.at[0], first(1)),
            comm.copy(b(self.i2, pl.ds(2, 2)), r1.at[1], first(3)),
        ]
        self.s2 = [
            comm.copy(b(self.i1, pl.ds(0, 4)), r2.at[0], first(1)),
            comm.copy(b(self.i3, pl.ds(0, 4)), r2.at[1], first(3)),
        ]
        self.s3 = [
            comm.copy(b(i, self.j2, pl.ds(0, h)), r3.at[0], second(1)),
            comm.copy(b(i, self.j2, pl.ds(h, h)), r3.at[1], second(3)),
        ]
        self.s4 = [
            comm.copy(b(i, self.j1), r4.at[0], second(1)),
            comm.copy(b(i, self.j3), r4.at[1], second(3)),
        ]

    def index(self, i, j):
        return (i, j) if self.y_first else (j, i)

    def block(self, i, j, rows=None):
        index = self.index(i, j)
        return self.buf.at[index] if rows is None else self.buf.at[index + (rows,)]

    def add(self, index, *others):
        total = self.buf[index].astype(F32)
        for other in others:
            total = total + other.astype(F32)
        self.buf[index] = total.astype(BF16)

    def step1(self):
        start(self.s1)

    def step2(self):
        arrived(self.s1)
        r1 = self.r[0]

        def body(k, _):
            self.add(self.index(self.i1, k), r1[0, k])
            self.add(self.index(self.i3, k + 2), r1[1, k])
            return 0

        lax.fori_loop(0, 2, body, 0)
        start(self.s2)

    def step3(self):
        arrived(self.s2)
        r2 = self.r[1]

        def body(k, _):
            self.add(self.index(self.i, k), r2[0, k], r2[1, k])
            return 0

        lax.fori_loop(0, 4, body, 0)
        start(self.s3)

    def step4(self):
        arrived(self.s3)
        r3 = self.r[2]
        h = self.rows // 2
        self.add(self.index(self.i, self.j1) + (pl.ds(0, h),), r3[0])
        self.add(self.index(self.i, self.j3) + (pl.ds(h, h),), r3[1])
        start(self.s4)

    def finish(self):
        arrived(self.s4)
        r4 = self.r[3]
        own = self.buf[self.index(self.i, self.j)].astype(F32)
        return own + r4[0].astype(F32) + r4[1].astype(F32)


def kernel(
    q_ref, k_ref, v_ref, g_ref, x_ref, gy_ref, ids_ref, rw_ref, w_ref, wd_ref, sink_ref, cos_ref, sin_ref,
    out_ref, dq_ref, dk_ref, dv_ref, ds_ref, moe_ref, dx_ref, dw_ref, dwd_ref,
    kb, vb, xb, yb, zs, zr, zs2, zr2, qz, qzt, gz, gzt, kk, vv, kt, vt, e_s, dp_s, m_s, ot, dqt,
    dka, dva, dkp, dvp, wg, wu, hid, dgu, py, px,
    ry1, ry2, ry3, ry4, rx1, rx2, rx3, rx4, rk1, rk2, rk3, rk4, rv1, rv2, rv3, rv4,
    rw, rwd, sx, sy, sz, sc,
    send, recv,
):
    cm = Comm(send, recv)
    me = cm.y * 4 + cm.x

    barrier = pltpu.get_barrier_semaphore()
    partners = [cm.at_x(k) for k in (1, 2, 3)] + [cm.at_y(k) for k in (1, 2, 3)]
    partners += [cm.at_z(k) for k in range(1, 8)] + [cm.at_c()]
    for where in partners:
        pl.semaphore_signal(barrier, inc=1, device_id=where, device_id_type=MESH)

    g_k, g_v = Gather(cm, kb, True), Gather(cm, vb, False)
    g_x, g_y = Gather(cm, xb, True), Gather(cm, yb, False)
    z_out = [
        cm.copy(zs.at[lax.rem(cm.z + k, 8)], zr.at[cm.z], cm.at_z(k)) for k in range(1, 8)
    ]
    z_back = [
        cm.copy(zs2.at[lax.rem(cm.z + k, 8)], zr2.at[cm.z], cm.at_z(k)) for k in range(1, 8)
    ]
    s_k, s_v = Scatter(cm, dka, True, rk1, rk2, rk3, rk4), Scatter(cm, dva, False, rv1, rv2, rv3, rv4)
    s_y, s_x = Scatter(cm, py, True, ry1, ry2, ry3, ry4), Scatter(cm, px, False, rx1, rx2, rx3, rx4)
    dw_out = [cm.copy(dw_ref, rw, cm.at_c()), cm.copy(dwd_ref, rwd, cm.at_c())]
    sink_x = [cm.copy(sx.at[cm.x], sx.at[cm.x], cm.at_x(k)) for k in (1, 2, 3)]
    sink_y = [cm.copy(sy.at[cm.y], sy.at[cm.y], cm.at_y(k)) for k in (1, 2, 3)]
    sink_z = [cm.copy(sz.at[cm.z], sz.at[cm.z], cm.at_z(k)) for k in range(1, 8)]
    sink_c = [cm.copy(sc.at[cm.c], sc.at[cm.c], cm.at_c())]

    lanes = lax.broadcasted_iota(jnp.int32, (128, 128), 1)
    subs = lax.broadcasted_iota(jnp.int32, (128, 128), 0)
    cos_t, sin_t = cos_ref[...], sin_ref[...]

    for t in range(2):
        part = k_ref[:, t * 128 : (t + 1) * 128].astype(F32)
        kb[cm.y, cm.x, :, t * 128 : (t + 1) * 128] = (
            part * cos_t + swap_halves(part, lanes) * sin_t
        ).astype(BF16)
    vb[cm.y, cm.x] = v_ref[...]

    expert, place = subs >> 4, subs & 15
    hit = jnp.zeros((128, 128), F32)
    share = jnp.zeros((128, 128), F32)
    for k in range(TOP):
        match = ids_ref[k : k + 1, :] == expert
        hit = jnp.where(match, 1.0, hit)
        share = share + jnp.where(match, rw_ref[k : k + 1, :], 0.0)
    upper = jnp.where(subs <= lanes, 1.0, 0.0).astype(BF16)
    rank = jnp.where(hit > 0.5, dot(hit.astype(BF16), upper), 0.0).astype(jnp.int32)
    pick_x = (rank == place + 1) & (place < CAP)
    pick_y = (rank == place - CAP + 1) & (place >= CAP) & (place < 2 * CAP)
    sel_x = jnp.where(pick_x, 1.0, 0.0).astype(BF16)
    sel_y = jnp.where(pick_y, 1.0, 0.0).astype(BF16)
    share_y = jnp.sum(jnp.where(pick_y, share, 0.0), axis=1, keepdims=True)
    share_x = jnp.where(pick_x, share, 0.0)
    zs[...] = (
        (dot(sel_x, x_ref[...], NT) + dot(sel_y, gy_ref[...], NT) * share_y)
        .astype(BF16)
        .reshape(8, 16, D)
    )
    zr[cm.z] = zs[cm.z]

    pl.semaphore_wait(barrier, len(partners))

    start(g_k.steps[0] + g_v.steps[0])
    start(z_out)

    def prepare(t, _):
        cut = pl.ds(pl.multiple_of(t * 128, 128), 128)
        part = q_ref[:, cut].astype(F32)
        part = (part * cos_t + swap_halves(part, lanes) * sin_t).astype(BF16).astype(F32)
        part = part * SCORE_SCALE
        grad = g_ref[:, cut].astype(F32)
        for p in range(2):
            rows = slice(p * 128, (p + 1) * 128)
            one = jnp.where((lanes >> 6) == p, part, 0.0)
            qz[t, rows, :] = one.astype(BF16)
            qzt[t, :, rows] = one.T.astype(BF16)
            one = jnp.where((lanes >> 6) == p, grad, 0.0)
            gz[t, rows, :] = one.astype(BF16)
            gzt[t, :, rows] = one.T.astype(BF16)
        return 0

    lax.fori_loop(0, 8, prepare, 0)
    arrived(g_k.steps[0] + g_v.steps[0])
    start(g_k.steps[1] + g_v.steps[1])
    lax.fori_loop(8, 16, prepare, 0)
    arrived(g_k.steps[1] + g_v.steps[1])
    start(g_k.steps[2] + g_v.steps[2])

    r_i = lax.broadcasted_iota(jnp.int32, (FFD, 2 * FFD), 0)
    c_i = lax.broadcasted_iota(jnp.int32, (FFD, 2 * FFD), 1)
    spread_g = jnp.where(c_i == 2 * r_i, 1.0, 0.0).astype(BF16)
    spread_u = jnp.where(c_i == 2 * r_i + 1, 1.0, 0.0).astype(BF16)
    wg[...] = dot(spread_g, w_ref[...]).astype(BF16)
    wu[...] = dot(spread_u, w_ref[...]).astype(BF16)

    def clear(k, _):
        dka[k // 4, lax.rem(k, 4)] = jnp.zeros((128, 256), BF16)
        dva[k // 4, lax.rem(k, 4)] = jnp.zeros((128, 256), BF16)
        return 0

    lax.fori_loop(0, 16, clear, 0)

    arrived(z_out)
    r_i = lax.broadcasted_iota(jnp.int32, (ROWS, 128), 0)
    c_i = lax.broadcasted_iota(jnp.int32, (ROWS, 128), 1)
    home = (r_i >> 2) * 16 + (r_i & 3)
    take_x = jnp.where(c_i == home, 1.0, 0.0).astype(BF16)
    take_y = jnp.where(c_i == home + CAP, 1.0, 0.0).astype(BF16)
    landed = zr[...].reshape(128, D)
    xb[cm.y, cm.x] = dot(take_x, landed).astype(BF16)
    yb[cm.y, cm.x] = dot(take_y, landed).astype(BF16)

    arrived(g_k.steps[2] + g_v.steps[2])
    start(g_k.steps[3] + g_v.steps[3])
    start(g_x.steps[0] + g_y.steps[0])
    arrived(g_k.steps[3] + g_v.steps[3])

    wide = me // 2 + 1
    key_in = lax.broadcasted_iota(jnp.int32, (256, 512), 0)
    query_in = lax.rem(lax.broadcasted_iota(jnp.int32, (256, 512), 1), 128)
    lanes2 = lax.broadcasted_iota(jnp.int32, (256, 128), 1)

    def attend(hh, _):
        group = hh // 2
        lane_cut = pl.ds(pl.multiple_of((group // 2) * 128, 128), 128)
        odd = lax.rem(group, 2)

        @pl.when(lax.rem(hh, 2) == 0)
        def _():
            def spread(j, _):
                rows = pl.ds(lax.rem(j, 2) * 2, 2)
                for source, twice, turned in ((kb, kk, kt), (vb, vv, vt)):
                    part = source[j // 2, rows, :, lane_cut].reshape(256, 128).astype(F32)
                    part = jnp.where((lanes2 >> 6) == odd, part, 0.0)
                    part = part + pltpu.roll(part, 64, 1)
                    twice[j] = part.astype(BF16)
                    turned[j] = part.T[:64].astype(BF16)
                dkp[j] = jnp.zeros((256, 128), F32)
                dvp[j] = jnp.zeros((256, 128), F32)
                return 0

            lax.fori_loop(0, wide, spread, 0)

        sink_row = jnp.concatenate(
            [jnp.full((1, 128), sink_ref[4 * hh + b], F32) for b in range(4)], axis=1
        )
        t0, t1 = 2 * hh, 2 * hh + 1

        def first(j, carry, masked):
            top, z_sum, d_sum = carry
            keys = kk[j]
            s = jnp.concatenate([dot(keys, qzt[t0]), dot(keys, qzt[t1])], axis=1)
            if masked:
                s = jnp.where(key_in + (j * 256 - me * 128) <= query_in, s, -1e30)
            new_top = jnp.maximum(top, jnp.max(s, axis=0, keepdims=True))
            keep = jnp.exp(top - new_top)
            e = jnp.exp(s - new_top)
            vals = vv[j]
            dp = jnp.concatenate([dot(vals, gzt[t0]), dot(vals, gzt[t1])], axis=1)
            e_s[j] = e
            dp_s[j] = dp
            m_s[j] = jnp.broadcast_to(new_top, (8, 512))
            z_sum = z_sum * keep + jnp.sum(e, axis=0, keepdims=True)
            d_sum = d_sum * keep + jnp.sum(e * dp, axis=0, keepdims=True)
            return new_top, z_sum, d_sum

        carry = (sink_row, jnp.ones((1, 512), F32), jnp.zeros((1, 512), F32))
        carry = lax.fori_loop(0, wide - 1, lambda j, c: first(j, c, False), carry)
        top, z_sum, d_sum = first(wide - 1, carry, True)
        inv = 1.0 / z_sum
        delta = d_sum * inv
        sx[cm.x, pl.ds(hh, 1), :] = -jnp.exp(sink_row - top) * inv * delta

        ot[...] = jnp.zeros((64, 512), F32)
        dqt[...] = jnp.zeros((64, 512), F32)

        def second(j, _):
            scale = jnp.exp(m_s[j][0:1] - top) * inv
            p = e_s[j] * scale
            pb = p.astype(BF16)
            ds = (p * (dp_s[j] - delta)).astype(BF16)
            dvp[j] += dot(pb[:, :256], gz[t0]) + dot(pb[:, 256:], gz[t1])
            dkp[j] += dot(ds[:, :256], qz[t0]) + dot(ds[:, 256:], qz[t1])
            ot[...] += dot(vt[j], pb)
            dqt[...] += dot(kt[j], ds)
            return 0

        lax.fori_loop(0, wide, second, 0)

        for i in range(2):
            cut = pl.ds(pl.multiple_of((2 * hh + i) * 128, 128), 128)
            lo, hi = slice(i * 256, i * 256 + 128), slice(i * 256 + 128, i * 256 + 256)
            out_ref[:, cut] = jnp.concatenate([ot[:, lo], ot[:, hi]], axis=0).T.astype(BF16)
            back = jnp.concatenate([dqt[:, lo], dqt[:, hi]], axis=0).T * SCORE_SCALE
            dq_ref[:, cut] = (back * cos_t - swap_halves(back, lanes) * sin_t).astype(BF16)

        @pl.when(lax.rem(hh, 2) == 1)
        def _():
            def collect(j, _):
                rows = pl.ds(lax.rem(j, 2) * 2, 2)
                for source, total in ((dkp, dka), (dvp, dva)):
                    part = source[j]
                    part = part + pltpu.roll(part, 64, 1)
                    part = jnp.where((lanes2 >> 6) == odd, part, 0.0)
                    old = total[j // 2, rows, :, lane_cut].reshape(256, 128).astype(F32)
                    total[j // 2, rows, :, lane_cut] = (old + part).astype(BF16).reshape(2, 128, 128)
                return 0

            lax.fori_loop(0, wide, collect, 0)

        for when, step in ((0, 0), (1, 1), (5, 2)):

            @pl.when(hh == when)
            def _(step=step):
                arrived(g_x.steps[step] + g_y.steps[step])
                start(g_x.steps[step + 1] + g_y.steps[step + 1])

        return 0

    lax.fori_loop(0, 8, attend, 0)

    s_k.step1()
    s_v.step1()
    start(sink_x)

    arrived(g_x.steps[3] + g_y.steps[3])

    def expert_rows(k, _):
        rows = xb[pl.ds(2 * k, 2)].reshape(256, D)
        grads = yb[pl.ds(2 * k, 2)].reshape(256, D)
        gate = dot(rows, wg[...], NT)
        up = dot(rows, wu[...], NT)
        dh = dot(grads, wd_ref[...], NT)
        sig = 1.0 / (1.0 + jnp.exp(-SWIGLU_ALPHA * gate))
        lift = sig * (up + 1.0)
        hid[pl.ds(2 * k, 2)] = (gate * lift).astype(BF16).reshape(2, 4, ROWS, FFD)
        dg = dh * lift * (1.0 + SWIGLU_ALPHA * gate * (1.0 - sig))
        du = dh * gate * sig
        both = dot(dg.astype(BF16), spread_g) + dot(du.astype(BF16), spread_u)
        dgu[pl.ds(2 * k, 2)] = both.astype(BF16).reshape(2, 4, ROWS, 2 * FFD)
        return 0

    lax.fori_loop(0, 2, expert_rows, 0)

    def y_rows(i):
        py[i] = dot(hid[i].reshape(128, FFD), wd_ref[...]).astype(BF16).reshape(4, ROWS, D)

    def x_rows(i):
        px[:, i] = dot(dgu[:, i].reshape(128, 2 * FFD), w_ref[...]).astype(BF16).reshape(4, ROWS, D)

    def chunk(k, _):
        y_rows(lax.rem(cm.y + k, 4))
        x_rows(lax.rem(cm.x + k, 4))
        return 0

    chunk(2, 0)
    s_y.step1()
    s_x.step1()
    s_k.step2()
    s_v.step2()
    lax.fori_loop(0, 2, lambda k, _: chunk(2 * k + 1, 0), 0)
    s_y.step2()
    s_x.step2()
    s_k.step3()
    s_v.step3()
    chunk(0, 0)

    arrived(sink_x)
    sy[cm.y] = ((sx[0] + sx[1]) + sx[2]) + sx[3]
    start(sink_y)

    turned = dgu[...].reshape(512, 2 * FFD).astype(F32).T.astype(BF16)
    turned_h = hid[...].reshape(512, FFD).astype(F32).T.astype(BF16)
    for lo in range(0, D, 512):
        cut = slice(lo, min(lo + 512, D))
        dw_ref[:, cut] = dot(turned, xb[:, :, :, cut].reshape(512, -1)).astype(BF16)
        dwd_ref[:, cut] = dot(turned_h, yb[:, :, :, cut].reshape(512, -1)).astype(BF16)
    start(dw_out)

    s_k.step4()
    s_v.step4()
    s_y.step3()
    s_x.step3()

    arrived(sink_y)
    sz[cm.z] = ((sy[0] + sy[1]) + sy[2]) + sy[3]
    start(sink_z)

    s_y.step4()
    s_x.step4()
    dk = s_k.finish()
    for t in range(2):
        part = dk[:, t * 128 : (t + 1) * 128]
        dk_ref[:, t * 128 : (t + 1) * 128] = (
            part * cos_t - swap_halves(part, lanes) * sin_t
        ).astype(BF16)
    dv_ref[...] = s_v.finish().astype(BF16)

    arrived(sink_z)
    total = sz[0]
    for k in range(1, 8):
        total = total + sz[k]
    sc[cm.c] = total
    start(sink_c)

    y_own = s_y.finish().astype(BF16)
    x_own = s_x.finish().astype(BF16)
    zs2[...] = (dot(take_x, y_own, TN) + dot(take_y, x_own, TN)).astype(BF16).reshape(8, 16, D)
    start(z_back)
    zr2[cm.z] = zs2[cm.z]

    arrived(dw_out)
    for made in dw_out:
        made.wait_send()
    for lo in range(0, D, 512):
        cut = slice(lo, min(lo + 512, D))
        dw_ref[:, cut] = (dw_ref[:, cut].astype(F32) + rw[:, cut].astype(F32)).astype(BF16)
        dwd_ref[:, cut] = (dwd_ref[:, cut].astype(F32) + rwd[:, cut].astype(F32)).astype(BF16)

    arrived(sink_c)
    ds_ref[...] = sc[0] + sc[1]

    arrived(z_back)
    back = zr2[...].reshape(128, D)
    high = share_x.astype(BF16)
    low = (share_x - high.astype(F32)).astype(BF16)
    moe_ref[...] = (dot(back, high, TN) + dot(back, low, TN)).astype(BF16)
    dx_ref[...] = dot(back, sel_y, TN).astype(BF16)

    for made in cm.all:
        if all(made is not other for other in dw_out):
            made.wait_send()


def own_tables(rows):
    steps_f = jnp.arange(HD // 2, dtype=F32)
    extrap_freq = 1.0 / jnp.exp(steps_f * (2.0 * math.log(ROPE_BASE) / HD))
    interp_freq = extrap_freq / YARN_FACTOR
    low_end = HD * math.log(YARN_INITIAL / (BETA_FAST * 2.0 * math.pi)) / (2.0 * math.log(ROPE_BASE))
    high_end = HD * math.log(YARN_INITIAL / (BETA_SLOW * 2.0 * math.pi)) / (2.0 * math.log(ROPE_BASE))
    ramp_val = jnp.clip((steps_f - low_end) / (high_end - low_end), 0.0, 1.0)
    inv_freq = interp_freq * ramp_val + extrap_freq * (1.0 - ramp_val)
    concentration = 0.1 * math.log(YARN_FACTOR) + 1.0
    at = (lax.axis_index("seq") * rows + jnp.arange(rows, dtype=jnp.int32)).astype(F32)
    angles = at[:, None] * jnp.tile(inv_freq, 4)[None, :]
    sign = jnp.where((jnp.arange(128) & 32) == 0, -concentration, concentration)
    return jnp.cos(angles) * concentration, jnp.sin(angles) * sign[None, :]


def body(query, keys, values, sinks, attn_grad, moe_in, moe_grad, expert_ids, route_weights, w_gate_up, w_down):
    rows = query.shape[1]
    cos_t, sin_t = own_tables(rows)
    vmem = pl.BlockSpec(memory_space=pltpu.VMEM)

    def v(*shape, dtype=BF16):
        return pltpu.VMEM(shape, dtype)

    def sums(r, c):
        return [v(2, 2, r, c), v(2, 4, r, c), v(2, r // 2, c), v(2, r, c)]

    scratch = [
        v(4, 4, 128, 256), v(4, 4, 128, 256), v(4, 4, ROWS, D), v(4, 4, ROWS, D),
        v(8, 16, D), v(8, 16, D), v(8, 16, D), v(8, 16, D),
        v(16, 256, 128), v(16, 128, 256), v(16, 256, 128), v(16, 128, 256),
        v(8, 256, 128), v(8, 256, 128), v(8, 64, 256), v(8, 64, 256),
        v(8, 256, 512, dtype=F32), v(8, 256, 512, dtype=F32), v(8, 8, 512, dtype=F32),
        v(64, 512, dtype=F32), v(64, 512, dtype=F32),
        v(4, 4, 128, 256), v(4, 4, 128, 256), v(8, 256, 128, dtype=F32), v(8, 256, 128, dtype=F32),
        v(FFD, D), v(FFD, D), v(4, 4, ROWS, FFD), v(4, 4, ROWS, 2 * FFD),
        v(4, 4, ROWS, D), v(4, 4, ROWS, D),
        *sums(ROWS, D), *sums(ROWS, D), *sums(128, 256), *sums(128, 256),
        v(2 * FFD, D), v(FFD, D),
        v(4, 8, 512, dtype=F32), v(4, 8, 512, dtype=F32), v(8, 8, 512, dtype=F32), v(2, 8, 512, dtype=F32),
        pltpu.SemaphoreType.DMA((96,)),
        pltpu.SemaphoreType.DMA((96,)),
    ]
    sds = jax.ShapeDtypeStruct
    outs = pl.pallas_call(
        kernel,
        out_shape=[
            sds((128, HQ * HD), BF16), sds((128, HQ * HD), BF16),
            sds((128, HK * HD), BF16), sds((128, HK * HD), BF16), sds((8, 512), F32),
            sds((D, 128), BF16), sds((D, 128), BF16), sds((2 * FFD, D), BF16), sds((FFD, D), BF16),
        ],
        in_specs=[vmem] * 10 + [pl.BlockSpec(memory_space=pltpu.SMEM)] + [vmem] * 2,
        out_specs=[vmem] * 9,
        scratch_shapes=scratch,
        compiler_params=pltpu.CompilerParams(
            collective_id=0, has_side_effects=True, vmem_limit_bytes=63 * 1024 * 1024
        ),
        name="layer",
    )(
        query[0], keys[0], values[0], attn_grad[0], moe_in[0].T, moe_grad[0].T,
        expert_ids[0].T, route_weights[0].T,
        jnp.transpose(w_gate_up[0], (2, 1, 0)).reshape(2 * FFD, D), w_down[0], sinks, cos_t, sin_t,
    )
    attn_out, d_query, d_keys, d_values, sink_sum, moe_out, d_moe_in, d_gate_up, d_down = outs
    d_sinks = jnp.sum(sink_sum.reshape(HQ, 128), axis=1)
    d_gate_up = jnp.transpose(d_gate_up.reshape(FFD, 2, D), (2, 1, 0))
    return (
        attn_out[None], d_query[None], d_keys[None], d_values[None], d_sinks,
        moe_out.T[None], d_moe_in.T[None], d_gate_up[None], d_down[None],
    )


def solution(mesh):
    rows = P(("dp", "exp"), "seq", None)
    gate_up, down = P("exp", None, None, "seq"), P("exp", "seq", None)
    return jax.shard_map(
        body,
        mesh=mesh,
        in_specs=(rows, rows, rows, P(), rows, rows, rows, rows, rows, gate_up, down),
        out_specs=(rows, rows, rows, rows, P(), rows, rows, gate_up, down),
        check_vma=False,
    )
```

time: 608 us -> 179 us (0.29); the launches traced: 601 us -> 179 us
  waiting for transfers between devices: 219 us -> 0 us
  Pallas kernels: 0 us -> 159 us
  matrix products: 116 us -> 0 us
  blocking collectives: 104 us -> 0 us
  local copies, waits for them, and re-layouts: 72.3 us -> 17.1 us
  other arithmetic: 37.7 us -> 1.62 us
  starting transfers between devices: 32.4 us -> 0 us
  between operations: 15.6 us -> 0.69 us
    pallas_call x0 -> x1, Pallas kernels: none -> 159 us  [body(): pl.pallas_call(kernel, out_shape=[sds((128, HQ * HD), BF16), sds((128, HQ...]
    all_gather x4 -> x0, waiting for transfers between devices: 122 us -> none  [the longest x1 52.2 us: body(): lax.all_gather(x_recv, 'seq', axis=0, tiled=True)]
    dot_general x34 -> x0, matrix products: 116 us -> none  [the longest x4 28.9 us: step_block(): jnp.einsum('hqk,qhd->kd', prob_b, g_block, preferred_element_type=jnp.flo...]
    psum x1 -> x0, blocking collectives: 73.8 us -> none  [body(): d_sinks = lax.psum(sink_vector, ('dp', 'seq', 'exp'))]
    all_to_all x6 -> x0, waiting for transfers between devices: 36.8 us -> none  [the longest x1 10.2 us: body(): lax.all_to_all(out_heads, 'seq', split_axis=0, concat_axis=1, tiled=True)]
    psum x1 -> x0, waiting for transfers between devices: 35.5 us -> none  [body(): lax.psum(d_gate_up_part.astype(jnp.bfloat16), 'dp').astype(jnp.float32)]
    all_to_all x6 -> x0, starting transfers between devices: 31.6 us -> none  [the longest x1 7.43 us: body(): lax.all_to_all(dx_own, 'exp', split_axis=0, concat_axis=0, tiled=True)]
    all_to_all x2 -> x0, blocking collectives: 30.1 us -> none  [the longest x1 17.3 us: body(): lax.all_to_all(x_send, 'exp', split_axis=0, concat_axis=0, tiled=True)]
  transfers between devices with their start and end apart: 14 -> 0, of which waited for: 10 -> 0; matrix products, arithmetic and copies ran while one was open for 31% -> 0% of each run, Pallas kernels for 0% -> 0%
where the time goes in v1:
time: 179 us
  Pallas kernels  159 us (89%)
  local copies, waits for them, and re-layouts  17.1 us (10%)
    pallas_call x1, Pallas kernels, body(): pl.pallas_call(kernel, out_shape=[sds((128, HQ * HD), BF16), sds((128, HQ...  159 us
    unnamed x21, local copies, waits for them, and re-layouts  5.58 us
    reshape x1, local copies, waits for them, and re-layouts, body(): jnp.transpose(w_gate_up[0], (2, 1, 0)).reshape(2 * FFD, D)  5.44 us
    reshape x1, local copies, waits for them, and re-layouts, body(): d_gate_up = jnp.transpose(d_gate_up.reshape(FFD, 2, D), (2, 1, 0))  5.32 us

profile of v1, /device:TPU:32, one launch (start us, length us, event | category | flops | bytes accessed | tf_op | source)
XLA Modules:
  0.0 178.8 jit_solution(17943488309753772201)
XLA Ops:
  0.7 0.1 mul.62
  0.8 1.0 fusion.1
  1.8 5.4 %reshape.54.w_ref = bf16[360,2880]{1,0:T(8,128)(2,1)} reshape(bf16[180,2,2880]{2,1,0:T(2,128)(2,1)} %bitcast.34) | data formatting | bytes 4147200 | tf_op jit(solution)/shard_map/reshape | solution.py:604
  7.2 159.3 %layer.1 = (bf16[128,2048]{1,0:T(8,128)(2,1)}, bf16[128,2048]{1,0:T(8,128)(2,1)}, bf16[128,256]{1,0:T(8,128)(2,1)}, bf16[128,256]{1,0:T(8,128)(2,1)}, f32[8,512]...) custom-call(bf16[128,2048]{1,0:T(8,128)(2,1)} %bitcast.44, ...), custom_call_target="tpu_custom_call" | custom-call | tf_op jit(solution)/shard_map/layer/pallas_call | solution.py:587
  166.5 0.7 reshape.55
  167.3 0.6 reduce_sum.9
  167.9 0.0 copy-start.4
  167.9 0.0 copy-start.3
  167.9 0.0 copy-start.6
  167.9 5.3 %reshape.56 = bf16[180,2,2880]{2,1,0:T(2,128)(2,1)} reshape(bf16[360,2880]{1,0:T(8,128)(2,1)} %get-tuple-element.25) | data formatting | bytes 4147200 | tf_op jit(solution)/shard_map/reshape | solution.py:608
  173.2 0.0 copy-start.5
  173.2 0.0 copy-start.2
  173.2 0.0 copy-start.1
  173.2 0.0 copy-done.4
  173.2 0.8 copy.27
  174.0 0.0 copy-done.3
  174.0 0.0 copy-start
  174.0 0.8 copy.28
  174.8 0.0 copy-done.6
  174.8 0.6 copy.29
  175.5 0.0 copy-done.5
  175.5 0.6 copy.30
  176.1 0.0 copy-done.2
  176.1 0.9 copy.31
  177.0 0.0 copy-done.1
  177.0 0.9 copy.32
  177.8 0.0 copy-done
  177.8 1.0 copy.33
  (4 shorter events, 0.0 us)
Async XLA Ops:
  167.9 5.3 %copy-start.4 = (bf16[128,2048]{1,0:T(8,128)(2,1)S(1)}, bf16[128,2048]{1,0:T(8,128)(2,1)}, u32[]{:S(2)}) copy-start(bf16[128,2048]{1,0:T(8,128)(2,1)} %get-tuple-element.18) | copy-start | bytes 1572868
  167.9 6.1 %copy-start.3 = (bf16[128,2048]{1,0:T(8,128)(2,1)S(1)}, bf16[128,2048]{1,0:T(8,128)(2,1)}, u32[]{:S(2)}) copy-start(bf16[128,2048]{1,0:T(8,128)(2,1)} %get-tuple-element.19) | copy-start | bytes 1572868
  167.9 6.9 %copy-start.6 = (bf16[128,256]{1,0:T(8,128)(2,1)S(1)}, bf16[128,256]{1,0:T(8,128)(2,1)}, u32[]{:S(2)}) copy-start(bf16[128,256]{1,0:T(8,128)(2,1)} %get-tuple-element.20) | copy-start | bytes 196612
  173.2 2.2 %copy-start.5 = (bf16[128,256]{1,0:T(8,128)(2,1)S(1)}, bf16[128,256]{1,0:T(8,128)(2,1)}, u32[]{:S(2)}) copy-start(bf16[128,256]{1,0:T(8,128)(2,1)} %get-tuple-element.21) | copy-start | bytes 196612
  173.2 2.9 %copy-start.2 = (bf16[2880,128]{1,0:T(8,128)(2,1)S(1)}, bf16[2880,128]{1,0:T(8,128)(2,1)}, u32[]{:S(2)}) copy-start(bf16[2880,128]{1,0:T(8,128)(2,1)} %get-tuple-element.23) | copy-start | bytes 2211844
  173.2 3.7 %copy-start.1 = (bf16[2880,128]{1,0:T(8,128)(2,1)S(1)}, bf16[2880,128]{1,0:T(8,128)(2,1)}, u32[]{:S(2)}) copy-start(bf16[2880,128]{1,0:T(8,128)(2,1)} %get-tuple-element.24) | copy-start | bytes 2211844
  174.0 3.8 %copy-start = (bf16[180,2880]{1,0:T(8,128)(2,1)S(1)}, bf16[180,2880]{1,0:T(8,128)(2,1)}, u32[]{:S(2)}) copy-start(bf16[180,2880]{1,0:T(8,128)(2,1)} %get-tuple-element.26) | copy-start | bytes 3110404

commit v2 on v1

v2 whole, which is shorter than its diff:
```python
import math

import jax
import jax.numpy as jnp
import numpy as np
from jax import lax
from jax.experimental import pallas as pl
from jax.experimental.pallas import tpu as pltpu
from jax.sharding import PartitionSpec as P

D = 2880
HQ = 32
HK = 4
HD = 64
TOP = 4
CAP = 4
FFD = 180
ROWS = 32
CUT = 1408
PIECE = D - CUT

ROPE_BASE = 150000.0
YARN_FACTOR = 32.0
YARN_INITIAL = 4096.0
BETA_FAST = 32.0
BETA_SLOW = 1.0
SWIGLU_ALPHA = 1.702
SCORE_SCALE = 0.125
CONCENTRATION = 0.1 * math.log(YARN_FACTOR) + 1.0

MESH = pl.DeviceIdType.MESH
F32 = jnp.float32
BF16 = jnp.bfloat16
NT = (((1,), (1,)), ((), ()))
TN = (((0,), (0,)), ((), ()))


def dot(a, b, dims=(((1,), (0,)), ((), ()))):
    return lax.dot_general(a, b, dims, preferred_element_type=F32)


def swap_halves(y, lanes):
    return jnp.where((lanes & 32) == 0, pltpu.roll(y, 96, 1), pltpu.roll(y, 32, 1))


class Comm:
    def __init__(self, send, recv):
        seq = lax.axis_index("seq")
        self.y, self.x = seq // 4, lax.rem(seq, 4)
        self.z = lax.axis_index("exp")
        self.c = lax.axis_index("dp")
        self.send, self.recv, self.used = send, recv, 0
        self.all = []

    def at_x(self, k):
        return {"seq": self.y * 4 + lax.rem(self.x + k, 4)}

    def at_y(self, k):
        return {"seq": lax.rem(self.y + k, 4) * 4 + self.x}

    def at_z(self, k):
        return {"exp": lax.rem(self.z + k, 8)}

    def at_c(self):
        return {"dp": 1 - self.c}

    def copy(self, src, dst, where):
        i = self.used
        self.used += 1
        made = pltpu.make_async_remote_copy(
            src_ref=src,
            dst_ref=dst,
            send_sem=self.send.at[i],
            recv_sem=self.recv.at[i],
            device_id=where,
            device_id_type=MESH,
        )
        self.all.append(made)
        return made


def start(copies):
    for made in copies:
        made.start()


def arrived(copies):
    for made in copies:
        made.wait_recv()


class Gather:
    def __init__(self, comm, buf, x_first):
        self.buf, self.x_first = buf, x_first
        self.rows = buf.shape[2]
        i, j = (comm.y, comm.x) if x_first else (comm.x, comm.y)
        near, far = (comm.at_x, comm.at_y) if x_first else (comm.at_y, comm.at_x)
        h = self.rows // 2
        jl, jr = lax.rem(j + 3, 4), lax.rem(j + 1, 4)
        il, ir = lax.rem(i + 3, 4), lax.rem(i + 1, 4)
        low, high = pl.ds(0, h), pl.ds(h, h)
        b = self.block
        self.steps = [
            [comm.copy(b(i, j), b(i, j), near(1)), comm.copy(b(i, j), b(i, j), near(3))],
            [
                comm.copy(b(i, jl, low), b(i, jl, low), near(1)),
                comm.copy(b(i, jr, high), b(i, jr, high), near(3)),
            ],
            [
                comm.copy(b(i, pl.ds(0, 4)), b(i, pl.ds(0, 4)), far(1)),
                comm.copy(b(i, pl.ds(0, 4)), b(i, pl.ds(0, 4)), far(3)),
            ],
            [
                comm.copy(b(il, pl.ds(0, 2)), b(il, pl.ds(0, 2)), far(1)),
                comm.copy(b(ir, pl.ds(2, 2)), b(ir, pl.ds(2, 2)), far(3)),
            ],
        ]

    def block(self, i, j, rows=None):
        index = (i, j) if self.x_first else (j, i)
        return self.buf.at[index] if rows is None else self.buf.at[index + (rows,)]


class Scatter:
    def __init__(self, comm, buf, y_first, r1, r2, r3, r4):
        self.buf, self.y_first = buf, y_first
        self.rows = buf.shape[2]
        i, j = (comm.y, comm.x) if y_first else (comm.x, comm.y)
        first, second = (comm.at_y, comm.at_x) if y_first else (comm.at_x, comm.at_y)
        self.i, self.j = i, j
        self.r = (r1, r2, r3, r4)
        h = self.rows // 2
        self.i1, self.i2, self.i3 = (lax.rem(i + k, 4) for k in (1, 2, 3))
        self.j1, self.j2, self.j3 = (lax.rem(j + k, 4) for k in (1, 2, 3))
        b = self.block
        self.s1 = [
            comm.copy(b(self.i2, pl.ds(0, 2)), r1.at[0], first(1)),
            comm.copy(b(self.i2, pl.ds(2, 2)), r1.at[1], first(3)),
        ]
        self.s2 = [
            comm.copy(b(self.i1, pl.ds(0, 4)), r2.at[0], first(1)),
            comm.copy(b(self.i3, pl.ds(0, 4)), r2.at[1], first(3)),
        ]
        self.s3 = [
            comm.copy(b(i, self.j2, pl.ds(0, h)), r3.at[0], second(1)),
            comm.copy(b(i, self.j2, pl.ds(h, h)), r3.at[1], second(3)),
        ]
        self.s4 = [
            comm.copy(b(i, self.j1), r4.at[0], second(1)),
            comm.copy(b(i, self.j3), r4.at[1], second(3)),
        ]

    def index(self, i, j):
        return (i, j) if self.y_first else (j, i)

    def block(self, i, j, rows=None):
        index = self.index(i, j)
        return self.buf.at[index] if rows is None else self.buf.at[index + (rows,)]

    def add(self, index, *others):
        total = self.buf[index].astype(F32)
        for other in others:
            total = total + other.astype(F32)
        self.buf[index] = total.astype(BF16)

    def step1(self):
        start(self.s1)

    def step2(self):
        arrived(self.s1)
        r1 = self.r[0]

        def body(k, _):
            self.add(self.index(self.i1, k), r1[0, k])
            self.add(self.index(self.i3, k + 2), r1[1, k])
            return 0

        lax.fori_loop(0, 2, body, 0)
        start(self.s2)

    def step3(self):
        arrived(self.s2)
        r2 = self.r[1]

        def body(k, _):
            self.add(self.index(self.i, k), r2[0, k], r2[1, k])
            return 0

        lax.fori_loop(0, 4, body, 0)
        start(self.s3)

    def step4(self):
        arrived(self.s3)
        r3 = self.r[2]
        h = self.rows // 2
        self.add(self.index(self.i, self.j1) + (pl.ds(0, h),), r3[0])
        self.add(self.index(self.i, self.j3) + (pl.ds(h, h),), r3[1])
        start(self.s4)

    def finish(self):
        arrived(self.s4)
        r4 = self.r[3]
        own = self.buf[self.index(self.i, self.j)].astype(F32)
        return own + r4[0].astype(F32) + r4[1].astype(F32)


def kernel(
    q_in, k_ref, v_ref, g_in, x_in, gy_in, ids_ref, rw_ref, w_in, wd_in, sink_ref, freq_ref,
    out_hbm, dq_hbm, dk_ref, dv_ref, ds_ref, z_hbm, share_ref, one_ref, dw_hbm, dwd_hbm,
    out_ref, dq_ref, x_ref, gy_ref, w3, wd_ref, wi,
    kb, vb, xb, yb, zs, zr, zs2, zr2, qz, qzt, gz, gzt, kk, vv, kt, vt, e_s, dp_s, m_s, st, ot, dqt,
    dka0, dka1, dva0, dva1, dkp, dvp, wg, wgt, wut, wdt, hid, dgu, py, px,
    ry1, ry2, ry3, ry4, rx1, rx2, rx3, rx4, k01, k02, k03, k04, k11, k12, k13, k14, v01, v02, v03, v04, v11, v12, v13, v14,
    rw, rwd, sx, sy, sz, sc,
    send, recv, local,
):
    cm = Comm(send, recv)
    me = cm.y * 4 + cm.x

    barrier = pltpu.get_barrier_semaphore()
    partners = [cm.at_x(k) for k in (1, 2, 3)] + [cm.at_y(k) for k in (1, 2, 3)]
    partners += [cm.at_z(k) for k in range(1, 8)] + [cm.at_c()]
    for where in partners:
        pl.semaphore_signal(barrier, inc=1, device_id=where, device_id_type=MESH)

    pairs = ((x_in, x_ref), (gy_in, gy_ref), (q_in, out_ref), (g_in, dq_ref), (w_in, w3), (wd_in, wd_ref))
    loads = [pltpu.make_async_copy(a, b, local.at[i]) for i, (a, b) in enumerate(pairs)]
    for load in loads:
        load.start()
    pairs = (
        (out_ref, out_hbm), (dq_ref, dq_hbm), (zr2, z_hbm), (w3, dw_hbm), (wd_ref, dwd_hbm),
    )
    stores = [pltpu.make_async_copy(a, b, local.at[6 + i]) for i, (a, b) in enumerate(pairs)]
    out_store, dq_store, z_store, dw_store, dwd_store = stores

    g_k, g_v = Gather(cm, kb, True), Gather(cm, vb, False)
    g_x, g_y = Gather(cm, xb, True), Gather(cm, yb, False)
    z_out = [
        cm.copy(zs.at[lax.rem(cm.z + k, 8)], zr.at[cm.z], cm.at_z(k)) for k in range(1, 8)
    ]
    z_back = [
        cm.copy(zs2.at[lax.rem(cm.z + k, 8)], zr2.at[cm.z], cm.at_z(k)) for k in range(1, 8)
    ]
    s_kv = [
        (Scatter(cm, dka0, True, k01, k02, k03, k04), Scatter(cm, dva0, False, v01, v02, v03, v04)),
        (Scatter(cm, dka1, True, k11, k12, k13, k14), Scatter(cm, dva1, False, v11, v12, v13, v14)),
    ]
    s_y, s_x = Scatter(cm, py, True, ry1, ry2, ry3, ry4), Scatter(cm, px, False, rx1, rx2, rx3, rx4)
    dw_out = [cm.copy(wi, rw, cm.at_c()), cm.copy(wg, rwd, cm.at_c())]
    sink_x = [cm.copy(sx.at[cm.x], sx.at[cm.x], cm.at_x(k)) for k in (1, 2, 3)]
    sink_y = [cm.copy(sy.at[cm.y], sy.at[cm.y], cm.at_y(k)) for k in (1, 2, 3)]
    sink_z = [cm.copy(sz.at[cm.z], sz.at[cm.z], cm.at_z(k)) for k in range(1, 8)]
    sink_c = [cm.copy(sc.at[cm.c], sc.at[cm.c], cm.at_c())]

    lanes = lax.broadcasted_iota(jnp.int32, (128, 128), 1)
    subs = lax.broadcasted_iota(jnp.int32, (128, 128), 0)
    angles = (subs + me * 128).astype(F32) * freq_ref[...]
    cos_t = jnp.cos(angles) * CONCENTRATION
    sin_t = jnp.sin(angles) * jnp.where((lanes & 32) == 0, -CONCENTRATION, CONCENTRATION)

    for t in range(2):
        part = k_ref[:, t * 128 : (t + 1) * 128].astype(F32)
        kb[cm.y, cm.x, :, t * 128 : (t + 1) * 128] = (
            part * cos_t + swap_halves(part, lanes) * sin_t
        ).astype(BF16)
    vb[cm.y, cm.x] = v_ref[...]

    expert, place = subs >> 4, subs & 7
    hit = jnp.zeros((128, 128), F32)
    share = jnp.zeros((128, 128), F32)
    for k in range(TOP):
        match = ids_ref[k : k + 1, :] == expert
        hit = jnp.where(match, 1.0, hit)
        share = share + jnp.where(match, rw_ref[k : k + 1, :], 0.0)
    upper = jnp.where(subs <= lanes, 1.0, 0.0).astype(BF16)
    rank = jnp.where(hit > 0.5, dot(hit.astype(BF16), upper), 0.0).astype(jnp.int32)
    pick_x = (rank == place + 1) & (place < CAP)
    pick_y = (rank == place - CAP + 1) & (place >= CAP)
    one_x = jnp.where(pick_x, 1.0, 0.0)
    one_y = jnp.where(pick_y, 1.0, 0.0)
    share_y = jnp.sum(jnp.where(pick_y, share, 0.0), axis=1, keepdims=True)
    share_ref[...] = jnp.where(pick_x, share, 0.0)
    one_ref[...] = one_y
    is_low = (subs & 8) == 0

    def parts(table):
        low = jnp.where(is_low, table, 0.0)
        return low.astype(BF16), (table - low).astype(BF16)

    pl.semaphore_wait(barrier, len(partners))
    start(g_k.steps[0] + g_v.steps[0])

    for load in loads[:2]:
        load.wait()
    (x_low, x_high), (y_low, y_high) = parts(one_x), parts(one_y)
    picked = dot(x_low, x_ref[:PIECE], NT) + dot(x_high, x_ref[CUT:], NT)
    picked += (dot(y_low, gy_ref[:PIECE], NT) + dot(y_high, gy_ref[CUT:], NT)) * share_y
    zs[...] = picked.astype(BF16).reshape(8, 16, PIECE)
    start(z_out)
    zr[cm.z] = zs[cm.z]

    def prepare(t, _):
        cut = pl.ds(pl.multiple_of(t * 128, 128), 128)
        part = out_ref[:, cut].astype(F32)
        part = (part * cos_t + swap_halves(part, lanes) * sin_t).astype(BF16).astype(F32)
        part = part * SCORE_SCALE
        grad = dq_ref[:, cut].astype(F32)
        for p in range(2):
            rows = slice(p * 128, (p + 1) * 128)
            one = jnp.where((lanes >> 6) == p, part, 0.0)
            qz[t, rows, :] = one.astype(BF16)
            qzt[t, :, rows] = one.T.astype(BF16)
            one = jnp.where((lanes >> 6) == p, grad, 0.0)
            gz[t, rows, :] = one.astype(BF16)
            gzt[t, :, rows] = one.T.astype(BF16)
        return 0

    for load in loads[2:4]:
        load.wait()
    arrived(g_k.steps[0] + g_v.steps[0])
    start(g_k.steps[1] + g_v.steps[1])
    lax.fori_loop(0, 8, prepare, 0)
    arrived(g_k.steps[1] + g_v.steps[1])
    start(g_k.steps[2] + g_v.steps[2])
    lax.fori_loop(8, 16, prepare, 0)

    arrived(z_out)
    r_i = lax.broadcasted_iota(jnp.int32, (ROWS, 128), 0)
    c_i = lax.broadcasted_iota(jnp.int32, (ROWS, 128), 1)
    home = (r_i >> 2) * 16 + (r_i & 3)
    takes = [jnp.where(c_i == home + k, 1.0, 0.0).astype(BF16) for k in (0, 4, 8, 12)]
    landed = zr[...].reshape(128, PIECE)
    for own, low, high in ((xb, takes[0], takes[2]), (yb, takes[1], takes[3])):
        own[cm.y, cm.x] = jnp.concatenate(
            [dot(low, landed[:, :CUT]).astype(BF16), dot(high, landed).astype(BF16)], axis=1
        )

    arrived(g_k.steps[2] + g_v.steps[2])
    start(g_k.steps[3] + g_v.steps[3])
    start(g_x.steps[0] + g_y.steps[0])

    for load in loads[4:]:
        load.wait()
    wi[...] = w3[...].reshape(2 * FFD, D)
    r_i = lax.broadcasted_iota(jnp.int32, (FFD, 2 * FFD), 0)
    c_i = lax.broadcasted_iota(jnp.int32, (FFD, 2 * FFD), 1)
    spread_g = jnp.where(c_i == 2 * r_i, 1.0, 0.0).astype(BF16)
    spread_u = jnp.where(c_i == 2 * r_i + 1, 1.0, 0.0).astype(BF16)
    wgt[...] = dot(spread_g, wi[...]).T.astype(BF16)
    wut[...] = dot(spread_u, wi[...]).T.astype(BF16)
    wdt[...] = wd_ref[...].astype(F32).T.astype(BF16)

    def clear(k, _):
        for total in (dka0, dka1, dva0, dva1):
            total[k // 4, lax.rem(k, 4)] = jnp.zeros((128, 128), BF16)
        return 0

    lax.fori_loop(0, 16, clear, 0)
    arrived(g_k.steps[3] + g_v.steps[3])

    wide = me // 2 + 1
    key_in = lax.broadcasted_iota(jnp.int32, (256, 512), 0)
    query_in = lax.rem(lax.broadcasted_iota(jnp.int32, (256, 512), 1), 128)
    lanes2 = lax.broadcasted_iota(jnp.int32, (256, 128), 1)

    def lane_cut(group):
        return pl.ds(pl.multiple_of((group // 2) * 128, 128), 128), lax.rem(group, 2)

    def spread_keys(group):
        cut, odd = lane_cut(group)

        def spread(j, _):
            rows = pl.ds(lax.rem(j, 2) * 2, 2)
            for source, twice, turned in ((kb, kk, kt), (vb, vv, vt)):
                part = source[j // 2, rows, :, cut].reshape(256, 128).astype(F32)
                part = jnp.where((lanes2 >> 6) == odd, part, 0.0)
                part = part + pltpu.roll(part, 64, 1)
                twice[j] = part.astype(BF16)
                turned[j] = part.T[:64].astype(BF16)
            dkp[j] = jnp.zeros((256, 128), F32)
            dvp[j] = jnp.zeros((256, 128), F32)
            return 0

        lax.fori_loop(0, wide, spread, 0)

    def collect_keys(group, half):
        odd = lax.rem(group, 2)
        totals = ((dkp, (dka0, dka1)[half]), (dvp, (dva0, dva1)[half]))

        def collect(j, _):
            rows = pl.ds(lax.rem(j, 2) * 2, 2)
            for source, total in totals:
                part = source[j]
                part = part + pltpu.roll(part, 64, 1)
                part = jnp.where((lanes2 >> 6) == odd, part, 0.0)
                old = total[j // 2, rows].reshape(256, 128).astype(F32)
                total[j // 2, rows] = (old + part).astype(BF16).reshape(2, 128, 128)
            return 0

        lax.fori_loop(0, wide, collect, 0)

    def scores(hh):
        t0, t1 = 2 * hh, 2 * hh + 1
        sink_row = jnp.concatenate(
            [jnp.full((1, 128), sink_ref[4 * hh + b], F32) for b in range(4)], axis=1
        )

        def first(j, carry, masked):
            top, z_sum, d_sum = carry
            keys = kk[j]
            s = jnp.concatenate([dot(keys, qzt[t0]), dot(keys, qzt[t1])], axis=1)
            if masked:
                s = jnp.where(key_in + (j * 256 - me * 128) <= query_in, s, -1e30)
            new_top = jnp.maximum(top, jnp.max(s, axis=0, keepdims=True))
            keep = jnp.exp(top - new_top)
            e = jnp.exp(s - new_top)
            vals = vv[j]
            dp = jnp.concatenate([dot(vals, gzt[t0]), dot(vals, gzt[t1])], axis=1)
            e_s[j] = e
            dp_s[j] = dp
            m_s[j] = jnp.broadcast_to(new_top, (8, 512))
            z_sum = z_sum * keep + jnp.sum(e, axis=0, keepdims=True)
            d_sum = d_sum * keep + jnp.sum(e * dp, axis=0, keepdims=True)
            return new_top, z_sum, d_sum

        carry = (sink_row, jnp.ones((1, 512), F32), jnp.zeros((1, 512), F32))
        carry = lax.fori_loop(0, wide - 1, lambda j, c: first(j, c, False), carry)
        top, z_sum, d_sum = first(wide - 1, carry, True)
        inv = 1.0 / z_sum
        delta = d_sum * inv
        sx[cm.x, pl.ds(hh, 1), :] = -jnp.exp(sink_row - top) * inv * delta
        for k, row in enumerate((top, inv, delta)):
            st[k] = jnp.broadcast_to(row, (8, 512))

    def gradients(hh):
        t0 = 2 * hh
        top, inv, delta = (st[k][0:1] for k in range(3))
        ot[...] = jnp.zeros((64, 512), F32)
        dqt[...] = jnp.zeros((64, 512), F32)

        def second(j, _):
            scale = jnp.exp(m_s[j][0:1] - top) * inv
            p = e_s[j] * scale
            pb = p.astype(BF16)
            ds = (p * (dp_s[j] - delta)).astype(BF16)
            dvp[j] += dot(pb, gz[pl.ds(t0, 2)].reshape(512, 128))
            dkp[j] += dot(ds, qz[pl.ds(t0, 2)].reshape(512, 128))
            ot[...] += dot(vt[j], pb)
            dqt[...] += dot(kt[j], ds)
            return 0

        lax.fori_loop(0, wide, second, 0)

        for i in range(2):
            cut = pl.ds(pl.multiple_of((2 * hh + i) * 128, 128), 128)
            lo, hi = slice(i * 256, i * 256 + 128), slice(i * 256 + 128, i * 256 + 256)
            out_ref[:, cut] = jnp.concatenate([ot[:, lo], ot[:, hi]], axis=0).T.astype(BF16)
            back = jnp.concatenate([dqt[:, lo], dqt[:, hi]], axis=0).T * SCORE_SCALE
            dq_ref[:, cut] = (back * cos_t - swap_halves(back, lanes) * sin_t).astype(BF16)

    def attend(u, half, hooks):
        hh = u // 2
        pl.when(lax.rem(u, 4) == 0)(lambda: spread_keys(hh // 2))
        pl.when(lax.rem(u, 2) == 0)(lambda: scores(hh))
        pl.when(lax.rem(u, 2) == 1)(lambda: gradients(hh))
        pl.when(lax.rem(u, 4) == 3)(lambda: collect_keys(hh // 2, half))
        for when, hook in hooks:
            pl.when(u == when)(hook)
        return 0

    def gather_on(step):
        def hook():
            arrived(g_x.steps[step] + g_y.steps[step])
            start(g_x.steps[step + 1] + g_y.steps[step + 1])

        return hook

    hooks = ((0, gather_on(0)), (1, gather_on(1)), (5, gather_on(2)))
    lax.fori_loop(0, 8, lambda u, _: attend(u, 0, hooks), 0)

    def kv_on(half, name):
        getattr(s_kv[half][0], name)()
        getattr(s_kv[half][1], name)()

    kv_on(0, "step1")

    arrived(g_x.steps[3] + g_y.steps[3])

    def expert_rows(k, _):
        rows = xb[pl.ds(2 * k, 2)].reshape(256, D)
        grads = yb[pl.ds(2 * k, 2)].reshape(256, D)
        gate = dot(rows, wgt[...])
        up = dot(rows, wut[...])
        dh = dot(grads, wdt[...])
        sig = 1.0 / (1.0 + jnp.exp(-SWIGLU_ALPHA * gate))
        lift = sig * (up + 1.0)
        hid[pl.ds(2 * k, 2)] = (gate * lift).astype(BF16).reshape(2, 4, ROWS, FFD)
        dg = dh * lift * (1.0 + SWIGLU_ALPHA * gate * (1.0 - sig))
        du = dh * gate * sig
        both = dot(dg.astype(BF16), spread_g) + dot(du.astype(BF16), spread_u)
        dgu[pl.ds(2 * k, 2)] = both.astype(BF16).reshape(2, 4, ROWS, 2 * FFD)
        return 0

    lax.fori_loop(0, 2, expert_rows, 0)

    def y_rows(i):
        py[i] = dot(hid[i].reshape(128, FFD), wd_ref[...]).astype(BF16).reshape(4, ROWS, D)

    def x_rows(i):
        px[:, i] = dot(dgu[:, i].reshape(128, 2 * FFD), wi[...]).astype(BF16).reshape(4, ROWS, D)

    def chunk(k, _):
        y_rows(lax.rem(cm.y + k, 4))
        x_rows(lax.rem(cm.x + k, 4))
        return 0

    kv_on(0, "step2")
    chunk(2, 0)
    s_y.step1()
    s_x.step1()
    lax.fori_loop(0, 2, lambda k, _: chunk(2 * k + 1, 0), 0)
    chunk(0, 0)

    turned = dgu[...].reshape(512, 2 * FFD).astype(F32).T.astype(BF16)
    turned_h = hid[...].reshape(512, FFD).astype(F32).T.astype(BF16)
    for lo in range(0, D, 512):
        cut = slice(lo, min(lo + 512, D))
        wi[:, cut] = dot(turned, xb[:, :, :, cut].reshape(512, -1)).astype(BF16)
        wg[:, cut] = dot(turned_h, yb[:, :, :, cut].reshape(512, -1)).astype(BF16)
    start(dw_out)
    kv_on(0, "step3")

    def both_sums(name):
        def hook():
            getattr(s_y, name)()
            getattr(s_x, name)()

        return hook

    def send_back():
        y_own = s_y.finish().astype(BF16)
        x_own = s_x.finish().astype(BF16)
        returned = dot(takes[0], y_own[:, :PIECE], TN) + dot(takes[1], x_own[:, :PIECE], TN)
        returned += dot(takes[2], y_own[:, CUT:], TN) + dot(takes[3], x_own[:, CUT:], TN)
        zs2[...] = returned.astype(BF16).reshape(8, 16, PIECE)
        start(z_back)
        zr2[cm.z] = zs2[cm.z]

    hooks = (
        (8, both_sums("step2")), (8, lambda: kv_on(0, "step4")), (12, both_sums("step3")), (13, both_sums("step4")),
        (14, lambda: start(sink_x)),
    )
    lax.fori_loop(8, 16, lambda u, _: attend(u, 1, hooks), 0)

    kv_on(1, "step1")
    send_back()
    out_store.start()
    dq_store.start()
    arrived(sink_x)
    sy[cm.y] = ((sx[0] + sx[1]) + sx[2]) + sx[3]
    start(sink_y)
    kv_on(1, "step2")
    arrived(sink_y)
    sz[cm.z] = ((sy[0] + sy[1]) + sy[2]) + sy[3]
    start(sink_z)

    arrived(dw_out)
    for lo in range(0, D, 512):
        cut = slice(lo, min(lo + 512, D))
        total = wi[:, cut].astype(F32) + rw[:, cut].astype(F32)
        w3[:, :, cut] = total.astype(BF16).reshape(FFD, 2, -1)
        wd_ref[:, cut] = (wg[:, cut].astype(F32) + rwd[:, cut].astype(F32)).astype(BF16)
    dw_store.start()
    dwd_store.start()

    kv_on(1, "step3")
    arrived(sink_z)
    total = sz[0]
    for k in range(1, 8):
        total = total + sz[k]
    sc[cm.c] = total
    start(sink_c)
    kv_on(1, "step4")

    for t, (k_part, v_part) in enumerate(s_kv):
        cut = slice(t * 128, (t + 1) * 128)
        part = k_part.finish()
        dk_ref[:, cut] = (part * cos_t - swap_halves(part, lanes) * sin_t).astype(BF16)
        dv_ref[:, cut] = v_part.finish().astype(BF16)

    arrived(sink_c)
    total = sc[0] + sc[1]
    row8 = lax.broadcasted_iota(jnp.int32, (8, HQ), 0)
    lane8 = lax.broadcasted_iota(jnp.int32, (8, HQ), 1)
    sums = jnp.zeros((8, HQ), F32)
    for b in range(4):
        part = jnp.sum(total[:, b * 128 : (b + 1) * 128], axis=1, keepdims=True)
        sums = sums + jnp.where(lane8 == 4 * row8 + b, part, 0.0)
    ds_ref[...] = jnp.sum(sums, axis=0, keepdims=True)

    arrived(z_back)
    z_store.start()
    for made in cm.all:
        made.wait_send()
    for store in stores:
        store.wait()


def finish(*refs):
    (z_ref, share_ref, one_ref), refs = refs[:3], refs[3:]
    sources, (moe_hbm, dx_hbm), results, held = refs[:7], refs[7:9], refs[9:16], refs[16:23]
    moe, dx, sems = refs[23:]
    loads = [pltpu.make_async_copy(sources[i], held[i], sems.at[i]) for i in range(7)]
    stores = [pltpu.make_async_copy(held[i], results[i], sems.at[7 + i]) for i in range(7)]
    last = [pltpu.make_async_copy(moe, moe_hbm, sems.at[14]), pltpu.make_async_copy(dx, dx_hbm, sems.at[15])]
    for load in loads:
        load.start()

    low_rows = (lax.broadcasted_iota(jnp.int32, (128, 128), 0) & 8) == 0
    share = share_ref[...]
    top = share.astype(BF16).astype(F32)
    tables = []
    for table in (top, share - top, one_ref[...]):
        low = jnp.where(low_rows, table, 0.0)
        tables.append((low.astype(BF16), (table - low).astype(BF16)))
    where = ((0, 768, 0, 0), (768, 640, 768, 0), (0, 768, CUT, 1), (768, 704, CUT + 768, 1))
    for i in range(7):
        loads[i].wait()
        stores[i].start()
        if i < 4:
            lane, n, at, high = where[i]
            back = z_ref[:, :, lane : lane + n].reshape(128, n)
            moe[at : at + n] = (dot(back, tables[0][high], TN) + dot(back, tables[1][high], TN)).astype(BF16)
            dx[at : at + n] = dot(back, tables[2][high], TN).astype(BF16)
    for made in last:
        made.start()
    for made in stores + last:
        made.wait()


def frequencies():
    steps_f = np.arange(HD // 2, dtype=np.float32)
    extrap_freq = np.float32(1.0) / np.exp(steps_f * np.float32(2.0 * math.log(ROPE_BASE) / HD))
    interp_freq = extrap_freq / np.float32(YARN_FACTOR)
    low_end = HD * math.log(YARN_INITIAL / (BETA_FAST * 2.0 * math.pi)) / (2.0 * math.log(ROPE_BASE))
    high_end = HD * math.log(YARN_INITIAL / (BETA_SLOW * 2.0 * math.pi)) / (2.0 * math.log(ROPE_BASE))
    ramp_val = np.clip((steps_f - np.float32(low_end)) / np.float32(high_end - low_end), 0.0, 1.0)
    inv_freq = interp_freq * ramp_val + extrap_freq * (np.float32(1.0) - ramp_val)
    return jnp.asarray(np.tile(inv_freq, 4)[None, :], F32)


def body(query, keys, values, sinks, attn_grad, moe_in, moe_grad, expert_ids, route_weights, w_gate_up, w_down):
    rows = query.shape[1]
    vmem = pl.BlockSpec(memory_space=pltpu.VMEM)

    def v(*shape, dtype=BF16):
        return pltpu.VMEM(shape, dtype)

    def sums(r, c):
        return [v(2, 2, r, c), v(2, 4, r, c), v(2, r // 2, c), v(2, r, c)]

    scratch = [
        v(rows, HQ * HD), v(rows, HQ * HD), v(D, rows), v(D, rows), v(FFD, 2, D), v(FFD, D), v(2 * FFD, D),
        v(4, 4, 128, 256), v(4, 4, 128, 256), v(4, 4, ROWS, D), v(4, 4, ROWS, D),
        v(8, 16, PIECE), v(8, 16, PIECE), v(8, 16, PIECE), v(8, 16, PIECE),
        v(16, 256, 128), v(16, 128, 256), v(16, 256, 128), v(16, 128, 256),
        v(8, 256, 128), v(8, 256, 128), v(8, 64, 256), v(8, 64, 256),
        v(8, 256, 512, dtype=F32), v(8, 256, 512, dtype=F32), v(8, 8, 512, dtype=F32),
        v(3, 8, 512, dtype=F32), v(64, 512, dtype=F32), v(64, 512, dtype=F32),
        *[v(4, 4, 128, 128)] * 4, v(8, 256, 128, dtype=F32), v(8, 256, 128, dtype=F32),
        v(FFD, D), *[v(D, FFD)] * 3, v(4, 4, ROWS, FFD), v(4, 4, ROWS, 2 * FFD),
        v(4, 4, ROWS, D), v(4, 4, ROWS, D),
        *sums(ROWS, D), *sums(ROWS, D), *sums(128, 128) * 4,
        v(2 * FFD, D), v(FFD, D),
        v(4, 8, 512, dtype=F32), v(4, 8, 512, dtype=F32), v(8, 8, 512, dtype=F32), v(2, 8, 512, dtype=F32),
        pltpu.SemaphoreType.DMA((112,)),
        pltpu.SemaphoreType.DMA((112,)),
        pltpu.SemaphoreType.DMA((12,)),
    ]
    sds = jax.ShapeDtypeStruct
    attn = [
        sds((rows, HQ * HD), BF16), sds((rows, HQ * HD), BF16),
        sds((rows, HK * HD), BF16), sds((rows, HK * HD), BF16), sds((1, HQ), F32),
    ]
    weights = [sds((FFD, 2, D), BF16), sds((FFD, D), BF16)]
    back = [sds((8, 16, PIECE), BF16)] + [sds((128, rows), F32)] * 2
    token = [sds((D, rows), BF16)] * 2
    hbm = pl.BlockSpec(memory_space=pl.ANY)
    smem = pl.BlockSpec(memory_space=pltpu.SMEM)
    outs = pl.pallas_call(
        kernel,
        out_shape=attn + back + weights,
        in_specs=[hbm, vmem, vmem, hbm, hbm, hbm, vmem, vmem, hbm, hbm, smem, vmem],
        out_specs=[hbm, hbm, vmem, vmem, vmem, hbm, vmem, vmem, hbm, hbm],
        scratch_shapes=scratch,
        compiler_params=pltpu.CompilerParams(
            collective_id=0, has_side_effects=True, vmem_limit_bytes=63 * 1024 * 1024
        ),
        name="layer",
    )(
        query[0], keys[0], values[0], attn_grad[0], moe_in[0].T, moe_grad[0].T,
        expert_ids[0].T, route_weights[0].T,
        jnp.transpose(w_gate_up[0], (2, 1, 0)), w_down[0], sinks, frequencies(),
    )
    outs = pl.pallas_call(
        finish,
        out_shape=token + attn + weights,
        in_specs=[vmem] * 3 + [hbm] * 7,
        out_specs=[hbm] * 9,
        scratch_shapes=[v(*one.shape, dtype=one.dtype) for one in attn + weights + token]
        + [pltpu.SemaphoreType.DMA((16,))],
        compiler_params=pltpu.CompilerParams(vmem_limit_bytes=63 * 1024 * 1024),
        name="finish",
    )(*outs[5:8], *outs[:5], *outs[8:])
    moe_out, d_moe_in, attn_out, d_query, d_keys, d_values, d_sinks, d_gate_up, d_down = outs
    return (
        attn_out[None], d_query[None], d_keys[None], d_values[None], d_sinks.reshape(HQ),
        moe_out.T[None], d_moe_in.T[None], jnp.transpose(d_gate_up, (2, 1, 0))[None], d_down[None],
    )


def solution(mesh):
    rows = P(("dp", "exp"), "seq", None)
    gate_up, down = P("exp", None, None, "seq"), P("exp", "seq", None)
    return jax.shard_map(
        body,
        mesh=mesh,
        in_specs=(rows, rows, rows, P(), rows, rows, rows, rows, rows, gate_up, down),
        out_specs=(rows, rows, rows, rows, P(), rows, rows, gate_up, down),
        check_vma=False,
    )
```

time: 179 us -> 132 us (0.74)
  Pallas kernels: 159 us -> 131 us
  local copies, waits for them, and re-layouts: 17.1 us -> 0 us
    pallas_call x1 -> x2, Pallas kernels: 159 us -> 131 us  [the longest x1 125 us: body(): pl.pallas_call(kernel, out_shape=attn + back + weights, in_specs=[hbm, vm...]
    reshape x3 -> x0, local copies, waits for them, and re-layouts: 11.5 us -> none  [the longest x1 5.44 us: body(): jnp.transpose(w_gate_up[0], (2, 1, 0)).reshape(2 * FFD, D)]
    unnamed x21 -> x0, local copies, waits for them, and re-layouts: 5.58 us -> none
where the time goes in v2:
time: 132 us
  Pallas kernels  131 us (99%)
    pallas_call x1, Pallas kernels, body(): pl.pallas_call(kernel, out_shape=attn + back + weights, in_specs=[hbm, vm...  125 us
    pallas_call x1, Pallas kernels, body(): pl.pallas_call(finish, out_shape=token + attn + weights, in_specs=[vmem]...  5.9 us

profile of v2, /device:TPU:32, one launch (start us, length us, event | category | flops | bytes accessed | tf_op | source)
XLA Modules:
  0.0 131.5 jit_solution(4799404528280670094)
XLA Ops:
  0.6 124.8 %layer.1 = (bf16[128,2048]{1,0:T(8,128)(2,1)}, bf16[128,2048]{1,0:T(8,128)(2,1)}, bf16[128,256]{1,0:T(8,128)(2,1)}, bf16[128,256]{1,0:T(8,128)(2,1)}, f32[1,32]{...) custom-call(bf16[128,2048]{1,0:T(8,128)(2,1)} %bitcast.39, ...), custom_call_target="tpu_custom_call" | custom-call | tf_op jit(solution)/shard_map/layer/pallas_call | solution.py:690
  125.5 5.9 %finish.1 = (bf16[2880,128]{1,0:T(8,128)(2,1)}, bf16[2880,128]{1,0:T(8,128)(2,1)}, bf16[128,2048]{1,0:T(8,128)(2,1)}, bf16[128,2048]{1,0:T(8,128)(2,1)}, bf16[12...) custom-call(bf16[8,16,1472]{2,1,0:T(8,128)(2,1)} %get-tuple-element., ...), custom_call_target="tpu_custom_call" | custom-call | tf_op jit(solution)/shard_map/finish/pallas_call | solution.py:705

commit v3 on v2

--- a/solution.py
+++ b/solution.py
@@ -209,7 +209,7 @@
     out_hbm, dq_hbm, dk_ref, dv_ref, ds_ref, z_hbm, share_ref, one_ref, dw_hbm, dwd_hbm,
     out_ref, dq_ref, x_ref, gy_ref, w3, wd_ref, wi,
     kb, vb, xb, yb, zs, zr, zs2, zr2, qz, qzt, gz, gzt, kk, vv, kt, vt, e_s, dp_s, m_s, st, ot, dqt,
-    dka0, dka1, dva0, dva1, dkp, dvp, wg, wgt, wut, wdt, hid, dgu, py, px,
+    dka0, dka1, dva0, dva1, dkp, dvp, wg, wu, hid, dgu, py, px,
     ry1, ry2, ry3, ry4, rx1, rx2, rx3, rx4, k01, k02, k03, k04, k11, k12, k13, k14, v01, v02, v03, v04, v11, v12, v13, v14,
     rw, rwd, sx, sy, sz, sc,
     send, recv, local,
@@ -315,14 +315,16 @@
             gzt[t, :, rows] = one.T.astype(BF16)
         return 0
 
+    arrived(g_k.steps[0] + g_v.steps[0])
+    start(g_k.steps[1] + g_v.steps[1])
     for load in loads[2:4]:
         load.wait()
-    arrived(g_k.steps[0] + g_v.steps[0])
-    start(g_k.steps[1] + g_v.steps[1])
-    lax.fori_loop(0, 8, prepare, 0)
+    lax.fori_loop(0, 5, prepare, 0)
     arrived(g_k.steps[1] + g_v.steps[1])
     start(g_k.steps[2] + g_v.steps[2])
-    lax.fori_loop(8, 16, prepare, 0)
+    lax.fori_loop(5, 16, prepare, 0)
+    arrived(g_k.steps[2] + g_v.steps[2])
+    start(g_k.steps[3] + g_v.steps[3])
 
     arrived(z_out)
     r_i = lax.broadcasted_iota(jnp.int32, (ROWS, 128), 0)
@@ -335,8 +337,6 @@
             [dot(low, landed[:, :CUT]).astype(BF16), dot(high, landed).astype(BF16)], axis=1
         )
 
-    arrived(g_k.steps[2] + g_v.steps[2])
-    start(g_k.steps[3] + g_v.steps[3])
     start(g_x.steps[0] + g_y.steps[0])
 
     for load in loads[4:]:
@@ -346,9 +346,8 @@
     c_i = lax.broadcasted_iota(jnp.int32, (FFD, 2 * FFD), 1)
     spread_g = jnp.where(c_i == 2 * r_i, 1.0, 0.0).astype(BF16)
     spread_u = jnp.where(c_i == 2 * r_i + 1, 1.0, 0.0).astype(BF16)
-    wgt[...] = dot(spread_g, wi[...]).T.astype(BF16)
-    wut[...] = dot(spread_u, wi[...]).T.astype(BF16)
-    wdt[...] = wd_ref[...].astype(F32).T.astype(BF16)
+    wg[...] = dot(spread_g, wi[...]).astype(BF16)
+    wu[...] = dot(spread_u, wi[...]).astype(BF16)
 
     def clear(k, _):
         for total in (dka0, dka1, dva0, dva1):
@@ -358,10 +357,10 @@
     lax.fori_loop(0, 16, clear, 0)
     arrived(g_k.steps[3] + g_v.steps[3])
 
-    wide = me // 2 + 1
-    key_in = lax.broadcasted_iota(jnp.int32, (256, 512), 0)
-    query_in = lax.rem(lax.broadcasted_iota(jnp.int32, (256, 512), 1), 128)
-    lanes2 = lax.broadcasted_iota(jnp.int32, (256, 128), 1)
+    wide = me // 4 + 1
+    key_in = lax.broadcasted_iota(jnp.int32, (512, 512), 0)
+    query_in = lax.rem(lax.broadcasted_iota(jnp.int32, (512, 512), 1), 128)
+    lanes2 = lax.broadcasted_iota(jnp.int32, (512, 128), 1)
 
     def lane_cut(group):
         return pl.ds(pl.multiple_of((group // 2) * 128, 128), 128), lax.rem(group, 2)
@@ -370,15 +369,14 @@
         cut, odd = lane_cut(group)
 
         def spread(j, _):
-            rows = pl.ds(lax.rem(j, 2) * 2, 2)
             for source, twice, turned in ((kb, kk, kt), (vb, vv, vt)):
-                part = source[j // 2, rows, :, cut].reshape(256, 128).astype(F32)
+                part = source[j, :, :, cut].reshape(512, 128).astype(F32)
                 part = jnp.where((lanes2 >> 6) == odd, part, 0.0)
                 part = part + pltpu.roll(part, 64, 1)
                 twice[j] = part.astype(BF16)
                 turned[j] = part.T[:64].astype(BF16)
-            dkp[j] = jnp.zeros((256, 128), F32)
-            dvp[j] = jnp.zeros((256, 128), F32)
+            dkp[j] = jnp.zeros((512, 128), F32)
+            dvp[j] = jnp.zeros((512, 128), F32)
             return 0
 
         lax.fori_loop(0, wide, spread, 0)
@@ -388,13 +386,12 @@
         totals = ((dkp, (dka0, dka1)[half]), (dvp, (dva0, dva1)[half]))
 
         def collect(j, _):
-            rows = pl.ds(lax.rem(j, 2) * 2, 2)
             for source, total in totals:
                 part = source[j]
                 part = part + pltpu.roll(part, 64, 1)
                 part = jnp.where((lanes2 >> 6) == odd, part, 0.0)
-                old = total[j // 2, rows].reshape(256, 128).astype(F32)
-                total[j // 2, rows] = (old + part).astype(BF16).reshape(2, 128, 128)
+                old = total[j].reshape(512, 128).astype(F32)
+                total[j] = (old + part).astype(BF16).reshape(4, 128, 128)
             return 0
 
         lax.fori_loop(0, wide, collect, 0)
@@ -410,7 +407,7 @@
             keys = kk[j]
             s = jnp.concatenate([dot(keys, qzt[t0]), dot(keys, qzt[t1])], axis=1)
             if masked:
-                s = jnp.where(key_in + (j * 256 - me * 128) <= query_in, s, -1e30)
+                s = jnp.where(key_in + (j * 512 - me * 128) <= query_in, s, -1e30)
             new_top = jnp.maximum(top, jnp.max(s, axis=0, keepdims=True))
             keep = jnp.exp(top - new_top)
             e = jnp.exp(s - new_top)
@@ -475,7 +472,8 @@
 
         return hook
 
-    hooks = ((0, gather_on(0)), (1, gather_on(1)), (5, gather_on(2)))
+    gather_on(0)()
+    hooks = ((0, gather_on(1)), (5, gather_on(2)))
     lax.fori_loop(0, 8, lambda u, _: attend(u, 0, hooks), 0)
 
     def kv_on(half, name):
@@ -489,9 +487,9 @@
     def expert_rows(k, _):
         rows = xb[pl.ds(2 * k, 2)].reshape(256, D)
         grads = yb[pl.ds(2 * k, 2)].reshape(256, D)
-        gate = dot(rows, wgt[...])
-        up = dot(rows, wut[...])
-        dh = dot(grads, wdt[...])
+        gate = dot(rows, wg[...], NT)
+        up = dot(rows, wu[...], NT)
+        dh = dot(grads, wd_ref[...], NT)
         sig = 1.0 / (1.0 + jnp.exp(-SWIGLU_ALPHA * gate))
         lift = sig * (up + 1.0)
         hid[pl.ds(2 * k, 2)] = (gate * lift).astype(BF16).reshape(2, 4, ROWS, FFD)
@@ -547,7 +545,7 @@
         zr2[cm.z] = zs2[cm.z]
 
     hooks = (
-        (8, both_sums("step2")), (8, lambda: kv_on(0, "step4")), (12, both_sums("step3")), (13, both_sums("step4")),
+        (8, both_sums("step2")), (8, lambda: kv_on(0, "step4")), (13, both_sums("step3")), (14, both_sums("step4")),
         (14, lambda: start(sink_x)),
     )
     lax.fori_loop(8, 16, lambda u, _: attend(u, 1, hooks), 0)
@@ -612,7 +610,11 @@
     moe, dx, sems = refs[23:]
     loads = [pltpu.make_async_copy(sources[i], held[i], sems.at[i]) for i in range(7)]
     stores = [pltpu.make_async_copy(held[i], results[i], sems.at[7 + i]) for i in range(7)]
-    last = [pltpu.make_async_copy(moe, moe_hbm, sems.at[14]), pltpu.make_async_copy(dx, dx_hbm, sems.at[15])]
+    last = [
+        pltpu.make_async_copy(made.at[cut], place.at[cut], sems.at[14 + 2 * i + j])
+        for i, cut in enumerate((pl.ds(0, CUT), pl.ds(CUT, D - CUT)))
+        for j, (made, place) in enumerate(((moe, moe_hbm), (dx, dx_hbm)))
+    ]
     for load in loads:
         load.start()
 
@@ -624,16 +626,16 @@
         low = jnp.where(low_rows, table, 0.0)
         tables.append((low.astype(BF16), (table - low).astype(BF16)))
     where = ((0, 768, 0, 0), (768, 640, 768, 0), (0, 768, CUT, 1), (768, 704, CUT + 768, 1))
-    for i in range(7):
-        loads[i].wait()
-        stores[i].start()
-        if i < 4:
-            lane, n, at, high = where[i]
-            back = z_ref[:, :, lane : lane + n].reshape(128, n)
-            moe[at : at + n] = (dot(back, tables[0][high], TN) + dot(back, tables[1][high], TN)).astype(BF16)
-            dx[at : at + n] = dot(back, tables[2][high], TN).astype(BF16)
-    for made in last:
-        made.start()
+    for load, store in zip(loads, stores):
+        load.wait()
+        store.start()
+    for i, (lane, n, at, high) in enumerate(where):
+        back = z_ref[:, :, lane : lane + n].reshape(128, n)
+        moe[at : at + n] = (dot(back, tables[0][high], TN) + dot(back, tables[1][high], TN)).astype(BF16)
+        dx[at : at + n] = dot(back, tables[2][high], TN).astype(BF16)
+        if i % 2 == 1:
+            for made in last[i - 1 : i + 1]:
+                made.start()
     for made in stores + last:
         made.wait()
 
@@ -664,11 +666,11 @@
         v(4, 4, 128, 256), v(4, 4, 128, 256), v(4, 4, ROWS, D), v(4, 4, ROWS, D),
         v(8, 16, PIECE), v(8, 16, PIECE), v(8, 16, PIECE), v(8, 16, PIECE),
         v(16, 256, 128), v(16, 128, 256), v(16, 256, 128), v(16, 128, 256),
-        v(8, 256, 128), v(8, 256, 128), v(8, 64, 256), v(8, 64, 256),
-        v(8, 256, 512, dtype=F32), v(8, 256, 512, dtype=F32), v(8, 8, 512, dtype=F32),
+        v(4, 512, 128), v(4, 512, 128), v(4, 64, 512), v(4, 64, 512),
+        v(4, 512, 512, dtype=F32), v(4, 512, 512, dtype=F32), v(4, 8, 512, dtype=F32),
         v(3, 8, 512, dtype=F32), v(64, 512, dtype=F32), v(64, 512, dtype=F32),
-        *[v(4, 4, 128, 128)] * 4, v(8, 256, 128, dtype=F32), v(8, 256, 128, dtype=F32),
-        v(FFD, D), *[v(D, FFD)] * 3, v(4, 4, ROWS, FFD), v(4, 4, ROWS, 2 * FFD),
+        *[v(4, 4, 128, 128)] * 4, v(4, 512, 128, dtype=F32), v(4, 512, 128, dtype=F32),
+        v(FFD, D), v(FFD, D), v(4, 4, ROWS, FFD), v(4, 4, ROWS, 2 * FFD),
         v(4, 4, ROWS, D), v(4, 4, ROWS, D),
         *sums(ROWS, D), *sums(ROWS, D), *sums(128, 128) * 4,
         v(2 * FFD, D), v(FFD, D),
@@ -708,7 +710,7 @@
         in_specs=[vmem] * 3 + [hbm] * 7,
         out_specs=[hbm] * 9,
         scratch_shapes=[v(*one.shape, dtype=one.dtype) for one in attn + weights + token]
-        + [pltpu.SemaphoreType.DMA((16,))],
+        + [pltpu.SemaphoreType.DMA((18,))],
         compiler_params=pltpu.CompilerParams(vmem_limit_bytes=63 * 1024 * 1024),
         name="finish",
     )(*outs[5:8], *outs[:5], *outs[8:])

time: 132 us -> 126 us (0.955)
  Pallas kernels: 131 us -> 125 us
    pallas_call x1, Pallas kernels: 125 us -> 120 us  [body(): pl.pallas_call(kernel, out_shape=attn + back + weights, in_specs=[hbm, vm...]
where the time goes in v3:
time: 126 us
  Pallas kernels  125 us (99%)
    pallas_call x1, Pallas kernels, body(): pl.pallas_call(kernel, out_shape=attn + back + weights, in_specs=[hbm, vm...  120 us
    pallas_call x1, Pallas kernels, body(): pl.pallas_call(finish, out_shape=token + attn + weights, in_specs=[vmem]...  5.49 us

profile of v3, /device:TPU:32, one launch (start us, length us, event | category | flops | bytes accessed | tf_op | source)
XLA Modules:
  0.0 125.8 jit_solution(17175373861887458711)
XLA Ops:
  0.6 119.5 %layer.1 = (bf16[128,2048]{1,0:T(8,128)(2,1)}, bf16[128,2048]{1,0:T(8,128)(2,1)}, bf16[128,256]{1,0:T(8,128)(2,1)}, bf16[128,256]{1,0:T(8,128)(2,1)}, f32[1,32]{...) custom-call(bf16[128,2048]{1,0:T(8,128)(2,1)} %bitcast.39, ...), custom_call_target="tpu_custom_call" | custom-call | tf_op jit(solution)/shard_map/layer/pallas_call | solution.py:692
  120.2 5.5 %finish.1 = (bf16[2880,128]{1,0:T(8,128)(2,1)}, bf16[2880,128]{1,0:T(8,128)(2,1)}, bf16[128,2048]{1,0:T(8,128)(2,1)}, bf16[128,2048]{1,0:T(8,128)(2,1)}, bf16[12...) custom-call(bf16[8,16,1472]{2,1,0:T(8,128)(2,1)} %get-tuple-element., ...), custom_call_target="tpu_custom_call" | custom-call | tf_op jit(solution)/shard_map/finish/pallas_call | solution.py:707
